TPU v7x, 128 devices: a whole 4x4x4 slice. The times are simulated.
128 devices in a mesh: seq: 8 (over x, z_hi), head: 16 (over y, z_lo, core).
Axes of the slice: x: 4, y: 4, z: 4 (z_hi: 2, z_lo: 2; z = z_hi * 2 + z_lo), core: 2. Of those that a mesh axis runs over, the one named last changes fastest.
Arguments:
- queries: bfloat16 [8192, 8192], P('seq', 'head'), may hold values from -8 to 8
- keys: bfloat16 [8192, 1024], P('seq'), may hold values from -8 to 8
- values: bfloat16 [8192, 1024], P('seq'), may hold values from -24 to 24
- w_out: bfloat16 [8192, 6144], P('head'), may hold values from -0.0625 to 0.0625
Outputs:
- mixed: bfloat16 [8192, 6144], P(('seq', 'head'))
All inputs are finite; a program needn't handle non-finite values.
Results may differ from a plain program's by a relative error of at most 0.023.
Values may be sent and summed in bfloat16 or wider, within the bound.
No kernel may reach another device: no remote copies, remote signals or barrier semaphores. Data moves between devices by JAX's collectives and lax.ppermute only.
A program may use at most 128 MiB of HBM per device.

v0:
```python
import jax
import jax.numpy as jnp
from jax import lax
from jax.sharding import PartitionSpec as P

HQ = 64
KV_HEADS = 8


NEG = -1e30


def project(attention, w_out):
    return lax.psum_scatter(
        jnp.dot(attention, w_out, preferred_element_type=jnp.float32).astype(jnp.bfloat16),
        "head",
        scatter_dimension=0,
        tiled=True,
    ).astype(jnp.float32)


def local(queries, keys, values, w_out):
    rows = queries.shape[0]
    head_dim = w_out.shape[0] // (
        queries.shape[1]
        // (queries.shape[1] // (w_out.shape[0] // (w_out.shape[0] // queries.shape[1])))
    )
    head_dim = queries.shape[1] * 0 + keys.shape[1] // KV_HEADS
    heads = queries.shape[1] // head_dim
    half = rows // 2
    place = lax.axis_index("seq")
    offsets = jnp.arange(rows, dtype=jnp.int32)
    scale = head_dim ** (-0.5)
    group_size = HQ // KV_HEADS
    slot = lax.axis_index("head") * heads // group_size
    slot_keys = lax.dynamic_slice_in_dim(keys, slot * head_dim, head_dim, 1)
    slot_values = lax.dynamic_slice_in_dim(values, slot * head_dim, head_dim, 1)
    positions = place * rows + offsets
    query_halves = queries.reshape(2, half, heads, head_dim)
    position_halves = positions.reshape(2, half)

    def update(state, query_heads, query_pos, key_block, value_block, first, masked):
        top, totals, summed = state
        width = key_block.shape[0]
        scores = (
            jnp.einsum("qhd,kd->qhk", query_heads, key_block, preferred_element_type=jnp.float32)
            * scale
        )
        if masked:
            key_pos = first + jnp.arange(width, dtype=jnp.int32)
            allowed = (key_pos[None, :] <= query_pos[:, None])[:, None, :]
            scores = jnp.where(allowed, scores, NEG)
        new_top = jnp.maximum(top, jnp.max(scores, axis=-1))
        weights = jnp.exp(scores - new_top[..., None])
        if masked:
            weights = jnp.where(allowed, weights, 0.0)
        fade = jnp.exp(top - new_top)
        totals = totals * fade + jnp.sum(weights, axis=-1)
        summed = summed * fade[..., None] + jnp.einsum(
            "qhk,kd->qhd",
            weights.astype(jnp.bfloat16),
            value_block,
            preferred_element_type=jnp.float32,
        )
        return (new_top, totals, summed)

    def advance(state, which, key_block, value_block, first):
        width = key_block.shape[0]
        query_heads = query_halves[which]
        query_pos = position_halves[which]
        lowest = query_pos[0]
        highest = query_pos[half - 1]
        branch = jnp.where(first > highest, 0, jnp.where(first + width - 1 <= lowest, 1, 2)).astype(
            jnp.int32
        )

        def keep(inner):
            return inner

        def plain(inner):
            return update(inner, query_heads, query_pos, key_block, value_block, first, False)

        def limited(inner):
            return update(inner, query_heads, query_pos, key_block, value_block, first, True)

        return lax.switch(branch, [keep, plain, limited], state)

    def fresh():
        return (
            jnp.full((half, heads), NEG, jnp.float32),
            jnp.zeros((half, heads), jnp.float32),
            jnp.zeros((half, heads, head_dim), jnp.float32),
        )

    state = (fresh(), fresh())
    key_piece = lax.all_gather(slot_keys, "seq", axis=0, tiled=True)
    value_piece = lax.all_gather(slot_values, "seq", axis=0, tiled=True)
    length = key_piece.shape[0]
    block = min(length, rows)
    count = length // block
    key_split = key_piece.reshape(count, block, head_dim)
    value_split = value_piece.reshape(count, block, head_dim)
    firsts = block * jnp.arange(count, dtype=jnp.int32)

    def step(inner, item):
        lower = advance(inner[0], 0, item[0], item[1], item[2])
        upper = advance(inner[1], 1, item[0], item[1], item[2])
        return ((lower, upper), None)

    state, _ = lax.scan(step, state, (key_split, value_split, firsts))
    lower, upper = state
    summed = jnp.concatenate([lower[2], upper[2]], axis=0)
    totals = jnp.concatenate([lower[1], upper[1]], axis=0)
    attention = (summed / totals[..., None]).astype(jnp.bfloat16).reshape(rows, heads * head_dim)
    mixed = project(attention, w_out).astype(jnp.bfloat16)
    return mixed


def solution(mesh):
    placed = (P("seq", "head"), P("seq", None), P("seq", None), P("head", None))
    return jax.shard_map(
        local, mesh=mesh, in_specs=placed, out_specs=P(("seq", "head"), None), check_vma=False
    )
```

profile of v0, /device:TPU:1, one launch (start us, length us, event | category | flops | bytes accessed | tf_op | source)
XLA Modules:
  0.0 439.3 jit_solution(18275301643613240672)
XLA Ops:
  6.5 1.6 copy-done
  8.1 0.8 constant_dynamic-slice_fusion.1
  9.0 1.7 constant_dynamic-slice_fusion
  10.7 1.3 reshape.92
  12.1 1.1 copy.6
  13.2 53.4 %all-gather.3.cloned.1.call-done = bf16[8192,128]{1,0:T(8,128)(2,1)} async-done(((bf16[1024,128]{1,0:T(8,128)(2,1)}), bf16[8192,128]{1,0:T(8,128)(2,1)}) %all-gather.3.cloned.1.call-update) | async-done | bytes 2097168 | tf_op jit(solution)/shard_map/all_gather | solution.py:96
  66.6 56.0 %all-gather.5.cloned.1.call-done = bf16[8192,128]{1,0:T(8,128)(2,1)} async-done(((bf16[1024,128]{1,0:T(8,128)(2,1)}), bf16[8192,128]{1,0:T(8,128)(2,1)}) %all-gather.5.cloned.1.call-update) | async-done | bytes 2097168 | tf_op jit(solution)/shard_map/all_gather | solution.py:97
  122.8 82.6 %while.24 = (s32[]{:T(128)}, f32[512,4]{0,1:T(4,128)S(1)}, f32[512,4]{0,1:T(4,128)S(1)}, f32[512,4,128]{2,0,1:T(8,128)S(1)}, f32[512,4]{0,1:T(4,128)S(1)}, /*ind...) while((s32[]{:T(128)}, f32[512,4]{0,1:T(4,128)S(1)}, ...), condition=%wide.region_15.16_spmd, body=%wide.region_0.15_spmd.sunk | while | flops 2204116992 | bytes 64254628 | solution.py:110
  122.8 0.6 dynamic_slice.44
  124.0 0.6 fusion.65
  128.4 1.1 dynamic-slice_bitcast_fusion.3
  129.5 1.3 slice_bitcast_fusion.3
  130.7 9.2 %conditional.5 = ((f32[512,4]{0,1:T(4,128)S(1)}, f32[512,4]{0,1:T(4,128)S(1)}, f32[512,4,128]{2,0,1:T(8,128)S(1)})) conditional(s32[]{:T(128)} %clamp.21, (f32[512,4]{0,1:T(4,128)S(1)}, f32[512,4]{0,1:T(4,128)S(1)}, f32[512,4,128]{2,0,1:T(8,128)S(1)}) %tuple.85, (bf16[512,4,128]{2,0,1:T(8,128)(2,1)S(1)}, ...), branch_computations={%region_8.8_spmd, %region_9.11_spmd, %region_12.14_spmd} | conditional | flops 1102058496 | bytes 30554148 | solution.py:86
  130.8 0.7 iota_add_fusion.1
  131.8 1.9 fusion.41
  133.7 3.0 fusion.43
  136.7 3.2 fusion.47
  139.9 9.1 %conditional.4 = ((f32[512,4]{0,1:T(4,128)S(1)}, f32[512,4]{0,1:T(4,128)S(1)}, f32[512,4,128]{2,0,1:T(8,128)S(1)})) conditional(s32[]{:T(128)} %clamp.20, (f32[512,4]{0,1:T(4,128)S(1)}, f32[512,4]{0,1:T(4,128)S(1)}, f32[512,4,128]{2,0,1:T(8,128)S(1)}) %tuple.82, (bf16[512,4,128]{2,0,1:T(8,128)(2,1)S(1)}, ...), branch_computations={%region_1.1_spmd, %region_2.4_spmd, %region_5.7_spmd} | conditional | flops 1102058496 | bytes 30554148 | solution.py:86
  140.0 0.7 iota_add_fusion
  141.0 1.8 fusion.13
  142.8 3.0 fusion.15
  145.9 3.2 fusion.19
  149.1 0.6 dynamic_slice.44
  150.3 0.6 fusion.65
  154.7 1.1 dynamic-slice_bitcast_fusion.3
  155.8 1.3 slice_bitcast_fusion.3
  157.1 0.6 dynamic_slice.44
  158.3 0.6 fusion.65
  162.7 1.1 dynamic-slice_bitcast_fusion.3
  163.8 1.3 slice_bitcast_fusion.3
  166.4 0.6 fusion.65
  170.7 1.1 dynamic-slice_bitcast_fusion.3
  171.8 1.3 slice_bitcast_fusion.3
  173.1 0.6 dynamic_slice.44
  174.4 0.6 fusion.65
  178.7 1.1 dynamic-slice_bitcast_fusion.3
  179.8 1.3 slice_bitcast_fusion.3
  182.4 0.6 fusion.65
  186.8 1.1 dynamic-slice_bitcast_fusion.3
  187.8 1.3 slice_bitcast_fusion.3
  190.4 0.6 fusion.65
  194.8 1.1 dynamic-slice_bitcast_fusion.3
  195.9 1.3 slice_bitcast_fusion.3
  198.4 0.6 fusion.65
  202.8 1.1 dynamic-slice_bitcast_fusion.3
  203.9 1.3 slice_bitcast_fusion.3
  206.4 12.6 %convolution_convert_fusion = bf16[1024,6144]{1,0:T(8,128)(2,1)} fusion(bf16[1024,512]{0,1:T(8,128)(2,1)S(1)} %fusion.56, bf16[512,6144]{1,0:T(8,128)(2,1)} %param.15), kind=kOutput, calls=%fused_computation.68 | convolution fusion | flops 6448742400 | bytes 19922944 | tf_op jit(solution)/shard_map/dot_general | solution.py:15
  219.0 213.8 %reduce-scatter.2.cloned.1.call-done = bf16[64,6144]{1,0:T(8,128)(2,1)} async-done(((bf16[1024,6144]{1,0:T(8,128)(2,1)}), bf16[64,6144]{1,0:T(8,128)(2,1)}) %reduce-scatter.2.cloned.1.call-update) | async-done | bytes 786448 | tf_op jit(solution)/shard_map/reduce_scatter | solution.py:14
  (49 shorter events, 4.6 us)
Async XLA Ops:
  6.5 1.6 copy-start
  6.5 60.1 %all-gather.3.cloned.1.call-start = ((), (), s32[]{:S(2)}) async-start(), calls=%async_computation.1 | async-start | bytes 2359296 | tf_op jit(solution)/shard_map/all_gather | solution.py:96
  8.9 113.7 %all-gather.5.cloned.1.call-start = ((), (), s32[]{:S(2)}) async-start(), calls=%async_computation.2 | async-start | bytes 2359296 | tf_op jit(solution)/shard_map/all_gather | solution.py:97
  10.7 422.1 %reduce-scatter.2.cloned.1.call-start = ((), (), s32[]{:S(2)}) async-start(), calls=%async_computation.3 | async-start | bytes 13369344 | tf_op jit(solution)/shard_map/reduce_scatter | solution.py:14
  206.3 226.5 %copy-start.1 = (bf16[1024,1024]{1,0:T(8,128)(2,1)S(1)}, bf16[1024,1024]{1,0:T(8,128)(2,1)}, u32[]{:S(2)}) copy-start(bf16[1024,1024]{1,0:T(8,128)(2,1)} %param.13) | copy-start | bytes 6291460
Sparse Core Ops, SparseCore 0:
  9.7 56.8 all-gather.2
  68.9 53.6 all-gather.4
  219.1 213.6 reduce-scatter.1
where the time goes:
time: 440 us; the launch traced here: 439 us
  waiting for transfers between devices  323 us (73%)
  loops' own time  36.3 us (8%)
  local copies, waits for them, and re-layouts  35.5 us (8%)
  matrix products  22.6 us (5%)
  between operations  13.2 us (3%)
  other arithmetic  8.38 us (2%)
    reduce_scatter x1, waiting for transfers between devices, project(): lax.psum_scatter(jnp.dot(attention, w_out, preferred_element_type=jnp.flo...  214 us
    all_gather x1, waiting for transfers between devices, local(): value_piece = lax.all_gather(slot_values, 'seq', axis=0, tiled=True)  56 us
    all_gather x1, waiting for transfers between devices, local(): key_piece = lax.all_gather(slot_keys, 'seq', axis=0, tiled=True)  53.4 us
    another operation x1, loops' own time, local(): state, _ = lax.scan(step, state, (key_split, value_split, firsts))  35.9 us
    dot_general x1, matrix products, project(): jnp.dot(attention, w_out, preferred_element_type=jnp.float32)  12.6 us
    squeeze x8, local copies, waits for them, and re-layouts, advance(): query_heads = query_halves[which]  10.2 us
  transfers between devices with their start and end apart: 3, of which 3 were waited for; matrix products, arithmetic and copies ran while one was open for 1% of the time, Pallas kernels for 0%

commit v1 on v0

v1 whole, which is shorter than its diff:
```python
import functools

import jax
import jax.numpy as jnp
from jax import lax
from jax.experimental import pallas as pl
from jax.experimental.pallas import tpu as pltpu
from jax.sharding import PartitionSpec as P

KV_HEADS = 8
DH = 128
LOG2E = 1.4426950408889634
NEG = -1e30
LIMIT = 60.0
CHUNKS = 4
BF = jnp.bfloat16
F32 = jnp.float32
VMEM_LIMIT = 56 << 20


def prep_kernel(info, k_ref, v_ref, ko_ref, vo_ref, mine_ref):
    k = k_ref[...]
    ko_ref[...] = k
    rows = k.shape[0]
    for t in range(rows // DH):
        vo_ref[t * DH : (t + 1) * DH, :] = v_ref[t * DH : (t + 1) * DH, :].T
    mine_ref[...] = jnp.where(info[2] == 0, k, vo_ref[...])


def prep(info, keys, values):
    rows = keys.shape[0]
    col = pl.BlockSpec((rows, DH), lambda i, info: (0, info[1]))
    whole = pl.BlockSpec((rows, DH), lambda i, info: (0, 0))
    shape = jax.ShapeDtypeStruct((rows, DH), BF)
    return pl.pallas_call(
        prep_kernel,
        grid_spec=pltpu.PrefetchScalarGridSpec(
            num_scalar_prefetch=1, grid=(1,), in_specs=[col, col], out_specs=[whole] * 3
        ),
        out_shape=[shape] * 3,
        name="prep",
        compiler_params=pltpu.CompilerParams(vmem_limit_bytes=VMEM_LIMIT),
    )(info, keys, values)


def attend_kernel(
    chunk, blocks, info, q_ref, k_ref, v_ref, mine_ref, other_ref, o_ref,
    q_buf, k_buf, v_buf, qt_ref, acc_ref, m_ref, mx_ref, o_buf, sems,
):
    place, core = info[0], info[2]
    rows = k_ref.shape[0]
    groups, _, sub, width = q_ref.shape
    heads = width // DH
    qb = groups * sub
    cols = heads * qb
    half = cols // 2
    q_copy = pltpu.make_async_copy(q_ref.at[:, chunk], q_buf, sems.at[0, blocks])
    k_copy = pltpu.make_async_copy(k_ref, k_buf.at[0], sems.at[0, 0])
    v_copy = pltpu.make_async_copy(v_ref, v_buf.at[0], sems.at[1, 0])
    q_copy.start()
    k_copy.start()
    v_copy.start()

    def start(d):
        @pl.when(jnp.logical_and(d <= place, core == 0))
        def _():
            pltpu.make_async_copy(mine_ref.at[d - 1], k_buf.at[d], sems.at[0, d]).start()
            pltpu.make_async_copy(other_ref.at[d - 1], v_buf.at[d], sems.at[1, d]).start()

        @pl.when(jnp.logical_and(d <= place, core != 0))
        def _():
            pltpu.make_async_copy(other_ref.at[d - 1], k_buf.at[d], sems.at[0, d]).start()
            pltpu.make_async_copy(mine_ref.at[d - 1], v_buf.at[d], sems.at[1, d]).start()

    for d in range(1, blocks):
        start(d)
    q_copy.wait()
    for h in range(heads):
        qh = q_buf[:, :, h * DH : (h + 1) * DH].reshape(qb, DH).astype(F32) * (DH**-0.5 * LOG2E)
        high = qh.astype(BF)
        low = (qh - high.astype(F32)).astype(BF)
        qt_ref[0:DH, h * qb : (h + 1) * qb] = high.T
        qt_ref[DH : 2 * DH, h * qb : (h + 1) * qb] = low.T
    k_copy.wait()
    v_copy.wait()

    def keys_of(d):
        k = k_buf[d]
        return jnp.concatenate([k, k], axis=1)

    def values_of(d):
        tiles = [v_buf[d, t * DH : (t + 1) * DH, :] for t in range(rows // DH)]
        return jnp.concatenate([jnp.concatenate(tiles, axis=1), jnp.ones((16, rows), BF)], axis=0)

    def scores(kk, c0):
        return jnp.dot(kk, qt_ref[:, c0 : c0 + half], preferred_element_type=F32)

    kk, vt = keys_of(0), values_of(0)
    col = lax.broadcasted_iota(jnp.int32, (rows, half), 1) % qb
    pos = (col // sub) * (rows // groups) + chunk * sub + col % sub
    allowed = lax.broadcasted_iota(jnp.int32, (rows, half), 0) <= pos
    for c0 in (0, half):
        s = jnp.where(allowed, scores(kk, c0), NEG)
        m = jnp.max(s, axis=0, keepdims=True)
        m_ref[:, c0 : c0 + half] = jnp.broadcast_to(m, (8, half))
        acc_ref[0, :, c0 : c0 + half] = jnp.dot(vt, jnp.exp2(s - m).astype(BF), preferred_element_type=F32)

    def body(d, _):
        pltpu.make_async_copy(k_ref, k_buf.at[d], sems.at[0, d]).wait()
        pltpu.make_async_copy(v_ref, v_buf.at[d], sems.at[1, d]).wait()
        old, new = (d + 1) % 2, d % 2
        kk, vt = keys_of(d), values_of(d)
        for c0 in (0, half):
            s = scores(kk, c0)
            mx_ref[:, c0 : c0 + half] = jnp.max(s.reshape(rows // 8, 8, half), axis=0)
            p = jnp.exp2(s - m_ref[0:1, c0 : c0 + half]).astype(BF)
            acc_ref[new, :, c0 : c0 + half] = acc_ref[old, :, c0 : c0 + half] + jnp.dot(
                vt, p, preferred_element_type=F32
            )
        over = jnp.max(mx_ref[...] - m_ref[...])

        @pl.when(over > LIMIT)
        def _():
            for c0 in (0, half):
                m = m_ref[0:1, c0 : c0 + half]
                top = jnp.maximum(m, jnp.max(mx_ref[:, c0 : c0 + half], axis=0, keepdims=True))
                p = jnp.exp2(scores(kk, c0) - top).astype(BF)
                acc_ref[new, :, c0 : c0 + half] = acc_ref[old, :, c0 : c0 + half] * jnp.exp2(
                    m - top
                ) + jnp.dot(vt, p, preferred_element_type=F32)
                m_ref[:, c0 : c0 + half] = jnp.broadcast_to(top, (8, half))

        return 0

    lax.fori_loop(1, place + 1, body, 0)
    last = place % 2
    for h in range(heads):
        o = acc_ref[last, :, h * qb : (h + 1) * qb]
        o = (o[0:DH] / o[DH : DH + 1]).T.astype(BF)
        o_buf[:, h * DH : (h + 1) * DH] = o
    for a in range(groups // 4):
        for b in range(4):
            src = (a * 4 + b) * sub
            ra = (a + groups // 4 - info[3]) % (groups // 4)
            rb = b ^ info[4]
            dst = pl.multiple_of((ra * 4 + rb) * sub, sub)
            o_ref[pl.ds(dst, sub), :] = o_buf[src : src + sub, :]


def attend(info, q4, k, v, mine, other, chunk):
    rows = k.shape[0]
    blocks = mine.shape[0] + 1
    groups, _, sub, width = q4.shape
    qb = groups * sub
    cols = width // DH * qb
    any_space = pl.BlockSpec(memory_space=pl.ANY)
    return pl.pallas_call(
        functools.partial(attend_kernel, chunk, blocks),
        grid_spec=pltpu.PrefetchScalarGridSpec(
            num_scalar_prefetch=1,
            grid=(1,),
            in_specs=[any_space] * 5,
            out_specs=pl.BlockSpec((qb, width), lambda i, info: (0, 0)),
            scratch_shapes=[
                pltpu.VMEM((groups, sub, width), BF),
                pltpu.VMEM((blocks, rows, DH), BF),
                pltpu.VMEM((blocks, rows, DH), BF),
                pltpu.VMEM((2 * DH, cols), BF),
                pltpu.VMEM((2, DH + 16, cols), F32),
                pltpu.VMEM((8, cols), F32),
                pltpu.VMEM((8, cols), F32),
                pltpu.VMEM((qb, width), BF),
                pltpu.SemaphoreType.DMA((2, blocks + 1)),
            ],
        ),
        out_shape=jax.ShapeDtypeStruct((qb, width), BF),
        name="attend",
        cost_estimate=pl.CostEstimate(
            flops=4 * cols * rows * blocks * 2 * DH // 2, bytes_accessed=8 << 20, transcendentals=cols * rows * blocks // 2
        ),
        compiler_params=pltpu.CompilerParams(vmem_limit_bytes=VMEM_LIMIT),
    )(info, q4, k, v, mine, other)


def project_kernel(a_ref, b_ref, wa_ref, wb_ref, *outs):
    s = jnp.dot(a_ref[...], wa_ref[...], preferred_element_type=F32) + jnp.dot(
        b_ref[...], wb_ref[...], preferred_element_type=F32
    )
    n = s.shape[0] // len(outs)
    for i, o in enumerate(outs):
        o[...] = s[i * n : (i + 1) * n].astype(BF)


def project(info, mine, other, w, w_other, parts, tile=512):
    rows, width = mine.shape
    n = w_other.shape[1]

    def body(info, a, b, wa, wb, *outs):
        project_kernel(a, b, wa, wb, *outs)

    steps = n // tile
    whole = pl.BlockSpec((rows, width), lambda i, info: (0, 0))
    return pl.pallas_call(
        body,
        grid_spec=pltpu.PrefetchScalarGridSpec(
            num_scalar_prefetch=1,
            grid=(steps,),
            in_specs=[
                whole,
                whole,
                pl.BlockSpec((width, tile), lambda i, info: (0, info[2] * steps + i)),
                pl.BlockSpec((width, tile), lambda i, info: (0, i)),
            ],
            out_specs=[pl.BlockSpec((rows // parts, tile), lambda i, info: (0, i))] * parts,
        ),
        out_shape=[jax.ShapeDtypeStruct((rows // parts, n), BF)] * parts,
        name="project",
        cost_estimate=pl.CostEstimate(
            flops=4 * rows * width * n, bytes_accessed=4 * width * n + 4 * rows * n, transcendentals=0
        ),
        compiler_params=pltpu.CompilerParams(vmem_limit_bytes=VMEM_LIMIT),
    )(info, mine, other, w, w_other)


def local(queries, keys, values, w_out):
    n_seq, n_head = lax.axis_size("seq"), lax.axis_size("head")
    rows, width = queries.shape
    cols = w_out.shape[1]
    place = lax.axis_index("seq")
    head = lax.axis_index("head")
    core, y, z = head % 2, head // 4, head // 2 % 2
    n_y = n_head // 4
    info = jnp.stack([place, head * KV_HEADS // n_head, core, y, head % 4, z]).astype(jnp.int32)

    def to(f):
        return [(h, f(h // 4, h // 2 % 2, h % 2)) for h in range(n_head)]

    def at(y, z, c):
        return (y % n_y) * 4 + z * 2 + c

    swap_core = to(lambda y, z, c: at(y, z, 1 - c))
    swap_z = to(lambda y, z, c: at(y, 1 - z, c))
    by_y = {d: to(lambda y, z, c, d=d: at(y + d, z, c)) for d in range(1, n_y)}

    k, v, mine = prep(info, keys, values)
    sent = [
        lax.ppermute(mine, "seq", [(s, s + d) for s in range(n_seq - d)]) for d in range(1, n_seq)
    ]
    mine = jnp.stack(sent)
    other = lax.ppermute(mine, "head", swap_core)
    w_away = lax.dynamic_slice_in_dim(w_out, (1 - core) * (cols // 2), cols // 2, 1)
    w_other = lax.ppermute(w_away, "head", swap_core)

    sub = rows // n_head // CHUNKS
    q4 = queries.reshape(n_head, CHUNKS, sub, width)
    pieces = []
    for chunk in range(CHUNKS):
        out = attend(info, q4, k, v, mine, other, chunk)
        out_other = lax.ppermute(out, "head", swap_core)
        fixed = out_other.reshape(n_head // 2, 2, sub, width)[:, ::-1].reshape(out.shape)
        parts = project(info, out, fixed, w_out, w_other, n_y)
        got = [lax.ppermute(parts[d], "head", by_y[d]) for d in range(1, n_y)]
        total = parts[0].astype(F32)
        for g in got:
            total = total + g.astype(F32)
        total = total.reshape(2, 2 * sub, cols // 2)
        far = lax.ppermute(total[1].astype(BF), "head", swap_z)
        total = (total[0] + far.astype(F32)).astype(BF).reshape(2, sub, cols // 2)
        pieces.append(total)
    done = jnp.concatenate([p[0] for p in pieces], axis=0)
    away = jnp.concatenate([p[1] for p in pieces], axis=0)
    back = lax.ppermute(away, "head", swap_core)
    left = jnp.where(core == 0, done, back)
    right = jnp.where(core == 0, back, done)
    return jnp.concatenate([left, right], axis=1)


def solution(mesh):
    placed = (P("seq", "head"), P("seq", None), P("seq", None), P("head", None))
    return jax.shard_map(
        local, mesh=mesh, in_specs=placed, out_specs=P(("seq", "head"), None), check_vma=False
    )
```

time: 440 us -> 200 us (0.45)
  the two profiles are of different devices: /device:TPU:1 before, /device:TPU:79 now
where the time goes in v1:
time: 200 us; the launch traced here: 199 us
  Pallas kernels  83.3 us (42%)
  starting transfers between devices  54.5 us (27%)
  waiting for transfers between devices  41.3 us (21%)
  local copies, waits for them, and re-layouts  17 us (8%)
    pallas_call x4, Pallas kernels, attend(): pl.pallas_call(functools.partial(attend_kernel, chunk, blocks), grid_spec...  51.2 us
    pallas_call x4, Pallas kernels, project(): pl.pallas_call(body, grid_spec=pltpu.PrefetchScalarGridSpec(num_scalar_pr...  29.5 us
    ppermute x12, waiting for transfers between devices, local(): got = [lax.ppermute(parts[d], 'head', by_y[d]) for d in range(1, n_y)]  23.1 us
    ppermute x12, starting transfers between devices, local(): got = [lax.ppermute(parts[d], 'head', by_y[d]) for d in range(1, n_y)]  20.5 us
    ppermute x1, starting transfers between devices, local(): other = lax.ppermute(mine, 'head', swap_core)  13.7 us
    ppermute x7, waiting for transfers between devices, local(): lax.ppermute(mine, 'seq', [(s, s + d) for s in range(n_seq - d)])  12.8 us
    ppermute x7, starting transfers between devices, local(): lax.ppermute(mine, 'seq', [(s, s + d) for s in range(n_seq - d)])  9.01 us
    ppermute x4, starting transfers between devices, local(): far = lax.ppermute(total[1].astype(BF), 'head', swap_z)  6.9 us
  transfers between devices with their start and end apart: 30, of which 10 were waited for; matrix products, arithmetic and copies ran while one was open for 7% of the time, Pallas kernels for 37%

profile of v1, /device:TPU:79, one launch (start us, length us, event | category | flops | bytes accessed | tf_op | source)
XLA Modules:
  0.0 198.5 jit_solution(2396346768648746949)
XLA Ops:
  0.6 2.7 %prep.1 = (bf16[1024,128]{1,0:T(8,128)(2,1)}, bf16[1024,128]{1,0:T(8,128)(2,1)}, bf16[1024,128]{1,0:T(8,128)(2,1)}) custom-call(s32[6]{0:T(128)} %stack.51.info, bf16[1024,1024]{1,0:T(8,128)(2,1)} %k_ref.1, bf16[1024,1024]{1,0:T(8,128)(2,1)} %v_ref.1), custom_call_target="tpu_custom_call" | custom-call | tf_op jit(solution)/shard_map/prep/pallas_call | solution.py:35
  3.3 1.3 collective-permute-start
  4.6 1.3 collective-permute-start.1
  5.9 1.3 collective-permute-start.6
  7.2 1.3 collective-permute-start.5
  8.5 1.3 collective-permute-start.4
  9.8 4.3 %collective-permute-done = bf16[1024,128]{1,0:T(8,128)(2,1)S(1)} collective-permute-done((bf16[1024,128]{1,0:T(8,128)(2,1)}, bf16[1024,128]{1,0:T(8,128)(2,1)S(1)}, u32[]{:S(2)}, u32[]{:S(2)}) %collective-permute-start) | collective-permute-done | bytes 262176 | tf_op jit(solution)/shard_map/ppermute | solution.py:247
  14.0 1.3 collective-permute-start.2
  16.1 1.2 collective-permute-done.1
  17.3 1.3 collective-permute-start.3
  19.3 7.3 %collective-permute-done.2 = bf16[1024,128]{1,0:T(8,128)(2,1)S(1)} collective-permute-done((bf16[1024,128]{1,0:T(8,128)(2,1)}, bf16[1024,128]{1,0:T(8,128)(2,1)S(1)}, u32[]{:S(2)}, u32[]{:S(2)}) %collective-permute-start.2) | collective-permute-done | bytes 262176 | tf_op jit(solution)/shard_map/ppermute | solution.py:247
  28.7 0.7 bitcast_dynamic-update-slice_fusion.1
  30.2 13.7 %collective-permute-start.7 = (bf16[7,1024,128]{2,1,0:T(8,128)(2,1)}, bf16[7,1024,128]{2,1,0:T(8,128)(2,1)}, u32[]{:S(2)}, u32[]{:S(2)}) collective-permute-start(bf16[7,1024,128]{2,1,0:T(8,128)(2,1)} %bitcast_dynamic-update-slice_fusion.mine_ref), channel_id=1, source_target_pairs={{0,1},{1,0},{2,3},{3,2},{4,5},{5,4},{6,7},{7,6},{8,9},{9,8},{10,11... | collective-permute-start | bytes 5505032 | tf_op jit(solution)/shard_map/ppermute | solution.py:250
  43.9 3.7 %constant_dynamic-slice_fusion = bf16[512,3072]{1,0:T(8,128)(2,1)} fusion(bf16[512,6144]{1,0:T(8,128)(2,1)} %wa.7, s32[]{:T(128)S(6)} %select_n.47), kind=kLoop, calls=%fused_computation.28 | loop fusion | bytes 6291460 | tf_op jit(solution)/shard_map/dynamic_slice | solution.py:251
  47.6 12.8 %attend.4.a = bf16[256,512]{1,0:T(8,128)(2,1)} custom-call(s32[6]{0:T(128)} %stack.51.info, bf16[16,4,16,512]{3,2,1,0:T(8,128)(2,1)} %bitcast.34, bf16[1024,128]{1,0:T(8,128)(2,1)} %get-tuple-element.24.k_ref, bf16[1024,128]{1,0:T(8,128)(2,1)} %get-tuple-element.25.v_ref, bf16[7,1024,128]{2,1,0:T(8,128)(2,1)} %bitcast_dynamic-update-slice_fusion.mine_ref, ...), custom_call_target="tpu_custom_call" | custom-call | flops 4294967296 | bytes 8388608 | tf_op jit(solution)/shard_map/attend/pallas_call | solution.py:157
  61.0 12.8 %attend.5.a = bf16[256,512]{1,0:T(8,128)(2,1)} custom-call(s32[6]{0:T(128)} %stack.51.info, bf16[16,4,16,512]{3,2,1,0:T(8,128)(2,1)} %bitcast.35, bf16[1024,128]{1,0:T(8,128)(2,1)} %get-tuple-element.24.k_ref, bf16[1024,128]{1,0:T(8,128)(2,1)} %get-tuple-element.25.v_ref, bf16[7,1024,128]{2,1,0:T(8,128)(2,1)} %bitcast_dynamic-update-slice_fusion.mine_ref, ...), custom_call_target="tpu_custom_call" | custom-call | flops 4294967296 | bytes 8388608 | tf_op jit(solution)/shard_map/attend/pallas_call | solution.py:157
  74.1 12.8 %attend.6.a = bf16[256,512]{1,0:T(8,128)(2,1)} custom-call(s32[6]{0:T(128)} %stack.51.info, bf16[16,4,16,512]{3,2,1,0:T(8,128)(2,1)} %bitcast.36, bf16[1024,128]{1,0:T(8,128)(2,1)} %get-tuple-element.24.k_ref, bf16[1024,128]{1,0:T(8,128)(2,1)} %get-tuple-element.25.v_ref, bf16[7,1024,128]{2,1,0:T(8,128)(2,1)} %bitcast_dynamic-update-slice_fusion.mine_ref, ...), custom_call_target="tpu_custom_call" | custom-call | flops 4294967296 | bytes 8388608 | tf_op jit(solution)/shard_map/attend/pallas_call | solution.py:157
  87.4 12.8 %attend.7.a = bf16[256,512]{1,0:T(8,128)(2,1)} custom-call(s32[6]{0:T(128)} %stack.51.info, bf16[16,4,16,512]{3,2,1,0:T(8,128)(2,1)} %bitcast.37, bf16[1024,128]{1,0:T(8,128)(2,1)} %get-tuple-element.24.k_ref, bf16[1024,128]{1,0:T(8,128)(2,1)} %get-tuple-element.25.v_ref, bf16[7,1024,128]{2,1,0:T(8,128)(2,1)} %bitcast_dynamic-update-slice_fusion.mine_ref, ...), custom_call_target="tpu_custom_call" | custom-call | flops 4294967296 | bytes 8388608 | tf_op jit(solution)/shard_map/attend/pallas_call | solution.py:157
  101.1 1.7 rev.13
  102.8 1.7 rev.14
  104.5 1.7 rev.15
  106.2 1.6 copy-done
  107.8 7.3 %project.7 = (bf16[64,3072]{1,0:T(8,128)(2,1)}, bf16[64,3072]{1,0:T(8,128)(2,1)}, bf16[64,3072]{1,0:T(8,128)(2,1)}, bf16[64,3072]{1,0:T(8,128)(2,1)}) custom-call(s32[6]{0:T(128)} %stack.51.info, bf16[256,512]{1,0:T(8,128)(2,1)} %attend.7.a, bf16[256,512]{1,0:T(8,128)(2,1)} %bitcast.32, bf16[512,6144]{1,0:T(8,128)(2,1)} %wa.7, bf16[512,3072]{1,0:T(8,128)(2,1)} %copy-done), custom_call_target="tpu_custom_call" | custom-call | flops 1610612736 | bytes 9437184 | tf_op jit(solution)/shard_map/project/pallas_call | solution.py:203
  115.1 1.3 collective-permute-start.25
  116.4 1.8 collective-permute-start.26
  118.2 1.0 collective-permute-start.27
  119.2 7.4 %project.6 = (bf16[64,3072]{1,0:T(8,128)(2,1)}, bf16[64,3072]{1,0:T(8,128)(2,1)}, bf16[64,3072]{1,0:T(8,128)(2,1)}, bf16[64,3072]{1,0:T(8,128)(2,1)}) custom-call(s32[6]{0:T(128)} %stack.51.info, bf16[256,512]{1,0:T(8,128)(2,1)} %attend.6.a, bf16[256,512]{1,0:T(8,128)(2,1)} %bitcast.31, bf16[512,6144]{1,0:T(8,128)(2,1)} %wa.7, bf16[512,3072]{1,0:T(8,128)(2,1)} %copy-done), custom_call_target="tpu_custom_call" | custom-call | flops 1610612736 | bytes 9437184 | tf_op jit(solution)/shard_map/project/pallas_call | solution.py:203
  127.1 2.4 %collective-permute-start.21 = (bf16[64,3072]{1,0:T(8,128)(2,1)}, bf16[64,3072]{1,0:T(8,128)(2,1)S(1)}, u32[]{:S(2)}, u32[]{:S(2)}) collective-permute-start(bf16[64,3072]{1,0:T(8,128)(2,1)} %get-tuple-element.37), channel_id=1, source_target_pairs={{0,8},{1,9},{2,10},{3,11},{4,12},{5,13},{6,14},{7,15},{8,0},{9,1},... | collective-permute-start | bytes 1179656 | tf_op jit(solution)/shard_map/ppermute | solution.py:262
  129.4 7.4 %project.5 = (bf16[64,3072]{1,0:T(8,128)(2,1)}, bf16[64,3072]{1,0:T(8,128)(2,1)}, bf16[64,3072]{1,0:T(8,128)(2,1)}, bf16[64,3072]{1,0:T(8,128)(2,1)}) custom-call(s32[6]{0:T(128)} %stack.51.info, bf16[256,512]{1,0:T(8,128)(2,1)} %attend.5.a, bf16[256,512]{1,0:T(8,128)(2,1)} %bitcast.30, bf16[512,6144]{1,0:T(8,128)(2,1)} %wa.7, bf16[512,3072]{1,0:T(8,128)(2,1)} %copy-done), custom_call_target="tpu_custom_call" | custom-call | flops 1610612736 | bytes 9437184 | tf_op jit(solution)/shard_map/project/pallas_call | solution.py:203
  136.8 7.5 %project.4 = (bf16[64,3072]{1,0:T(8,128)(2,1)}, bf16[64,3072]{1,0:T(8,128)(2,1)}, bf16[64,3072]{1,0:T(8,128)(2,1)}, bf16[64,3072]{1,0:T(8,128)(2,1)}) custom-call(s32[6]{0:T(128)} %stack.51.info, bf16[256,512]{1,0:T(8,128)(2,1)} %attend.4.a, bf16[256,512]{1,0:T(8,128)(2,1)} %bitcast.29, bf16[512,6144]{1,0:T(8,128)(2,1)} %wa.7, bf16[512,3072]{1,0:T(8,128)(2,1)} %copy-done), custom_call_target="tpu_custom_call" | custom-call | flops 1610612736 | bytes 9437184 | tf_op jit(solution)/shard_map/project/pallas_call | solution.py:203
  144.7 1.4 collective-permute-start.15
  146.2 1.8 collective-permute-start.16
  148.4 3.7 %collective-permute-start.10 = (bf16[64,3072]{1,0:T(8,128)(2,1)S(1)}, bf16[64,3072]{1,0:T(8,128)(2,1)S(1)}, u32[]{:S(2)}, u32[]{:S(2)}) collective-permute-start(bf16[64,3072]{1,0:T(8,128)(2,1)S(1)} %copy-done.7), channel_id=1, source_target_pairs={{0,4},{1,5},{2,6},{3,7},{4,8},{5,9},{6,10},{7,11},{8,12},{9,13},{1... | collective-permute-start | bytes 1179656 | tf_op jit(solution)/shard_map/ppermute | solution.py:262
  152.1 1.8 collective-permute-done.22
  153.9 2.2 %collective-permute-start.11 = (bf16[64,3072]{1,0:T(8,128)(2,1)S(1)}, bf16[64,3072]{1,0:T(8,128)(2,1)S(1)}, u32[]{:S(2)}, u32[]{:S(2)}) collective-permute-start(bf16[64,3072]{1,0:T(8,128)(2,1)S(1)} %copy-done.6), channel_id=1, source_target_pairs={{0,8},{1,9},{2,10},{3,11},{4,12},{5,13},{6,14},{7,15},{8,0},{9,1},... | collective-permute-start | bytes 1179656 | tf_op jit(solution)/shard_map/ppermute | solution.py:262
  156.3 3.3 %collective-permute-done.15 = bf16[64,3072]{1,0:T(8,128)(2,1)S(1)} collective-permute-done((bf16[64,3072]{1,0:T(8,128)(2,1)S(1)}, bf16[64,3072]{1,0:T(8,128)(2,1)S(1)}, u32[]{:S(2)}, u32[]{:S(2)}) %collective-permute-start.15) | collective-permute-done | bytes 393248 | tf_op jit(solution)/shard_map/ppermute | solution.py:262
  159.6 3.9 %collective-permute-start.12 = (bf16[64,3072]{1,0:T(8,128)(2,1)S(1)}, bf16[64,3072]{1,0:T(8,128)(2,1)S(1)}, u32[]{:S(2)}, u32[]{:S(2)}) collective-permute-start(bf16[64,3072]{1,0:T(8,128)(2,1)S(1)} %copy-done.5), channel_id=1, source_target_pairs={{0,12},{1,13},{2,14},{3,15},{4,0},{5,1},{6,2},{7,3},{8,4},{9,5},{1... | collective-permute-start | bytes 1179656 | tf_op jit(solution)/shard_map/ppermute | solution.py:262
  163.5 1.4 collective-permute-start.28
  164.8 5.9 %collective-permute-done.17 = bf16[64,3072]{1,0:T(8,128)(2,1)S(1)} collective-permute-done((bf16[64,3072]{1,0:T(8,128)(2,1)S(1)}, bf16[64,3072]{1,0:T(8,128)(2,1)S(1)}, u32[]{:S(2)}, u32[]{:S(2)}) %collective-permute-start.17) | collective-permute-done | bytes 393248 | tf_op jit(solution)/shard_map/ppermute | solution.py:262
  170.7 1.3 collective-permute-start.23
  172.3 4.1 %collective-permute-done.10 = bf16[64,3072]{1,0:T(8,128)(2,1)S(1)} collective-permute-done((bf16[64,3072]{1,0:T(8,128)(2,1)S(1)}, bf16[64,3072]{1,0:T(8,128)(2,1)S(1)}, u32[]{:S(2)}, u32[]{:S(2)}) %collective-permute-start.10) | collective-permute-done | bytes 393248 | tf_op jit(solution)/shard_map/ppermute | solution.py:262
  176.4 2.8 %collective-permute-start.18 = (bf16[32,3072]{1,0:T(8,128)(2,1)S(1)}, bf16[32,3072]{1,0:T(8,128)(2,1)S(1)}, u32[]{:S(2)}, u32[]{:S(2)}) collective-permute-start(bf16[32,3072]{1,0:T(8,128)(2,1)S(1)} %slice.118), channel_id=1, source_target_pairs={{0,2},{1,3},{2,0},{3,1},{4,6},{5,7},{6,4},{7,5},{8,10},{9,11},{10,... | collective-permute-start | bytes 589832 | tf_op jit(solution)/shard_map/ppermute | solution.py:267
  179.2 7.9 %collective-permute-done.12 = bf16[64,3072]{1,0:T(8,128)(2,1)S(1)} collective-permute-done((bf16[64,3072]{1,0:T(8,128)(2,1)S(1)}, bf16[64,3072]{1,0:T(8,128)(2,1)S(1)}, u32[]{:S(2)}, u32[]{:S(2)}) %collective-permute-start.12) | collective-permute-done | bytes 393248 | tf_op jit(solution)/shard_map/ppermute | solution.py:262
  187.4 1.4 collective-permute-start.13
  189.0 4.1 %collective-permute-done.13 = bf16[32,3072]{1,0:T(8,128)(2,1)S(1)} collective-permute-done((bf16[32,3072]{1,0:T(8,128)(2,1)S(1)}, bf16[32,3072]{1,0:T(8,128)(2,1)S(1)}, u32[]{:S(2)}, u32[]{:S(2)}) %collective-permute-start.13) | collective-permute-done | bytes 196640 | tf_op jit(solution)/shard_map/ppermute | solution.py:267
  193.2 2.9 %collective-permute-start.29 = (bf16[64,3072]{1,0:T(8,128)(2,1)S(1)}, bf16[64,3072]{1,0:T(8,128)(2,1)S(1)}, u32[]{:S(2)}, u32[]{:S(2)}) collective-permute-start(bf16[64,3072]{1,0:T(8,128)(2,1)S(1)} %pad_maximum_fusion.2), channel_id=1, source_target_pairs={{0,1},{1,0},{2,3},{3,2},{4,5},{5,4},{6,7},{7,6},{8,9},{9,8},{10,11... | collective-permute-start | bytes 1179656 | tf_op jit(solution)/shard_map/ppermute | solution.py:272
  196.1 1.3 collective-permute-done.29
  197.6 0.9 pad_maximum_fusion
  (77 shorter events, 9.5 us)
Async XLA Ops:
  3.3 10.8 %collective-permute-start = (bf16[1024,128]{1,0:T(8,128)(2,1)}, bf16[1024,128]{1,0:T(8,128)(2,1)S(1)}, u32[]{:S(2)}, u32[]{:S(2)}) collective-permute-start(bf16[1024,128]{1,0:T(8,128)(2,1)} %get-tuple-element.26), channel_id=1, source_target_pairs={{0,16},{16,32},{32,48},{48,64},{64,80},{80,96},{96,112},{1,17},{17... | collective-permute-start | bytes 786440 | tf_op jit(solution)/shard_map/ppermute | solution.py:247
  4.6 12.7 %collective-permute-start.1 = (bf16[1024,128]{1,0:T(8,128)(2,1)}, bf16[1024,128]{1,0:T(8,128)(2,1)S(1)}, u32[]{:S(2)}, u32[]{:S(2)}) collective-permute-start(bf16[1024,128]{1,0:T(8,128)(2,1)} %get-tuple-element.26), channel_id=1, source_target_pairs={{0,32},{16,48},{32,64},{48,80},{64,96},{80,112},{1,33},{17,49},{33... | collective-permute-start | bytes 786440 | tf_op jit(solution)/shard_map/ppermute | solution.py:247
  5.9 23.6 %collective-permute-start.6 = (bf16[1024,128]{1,0:T(8,128)(2,1)}, bf16[1024,128]{1,0:T(8,128)(2,1)S(1)}, u32[]{:S(2)}, u32[]{:S(2)}) collective-permute-start(bf16[1024,128]{1,0:T(8,128)(2,1)} %get-tuple-element.26), channel_id=1, source_target_pairs={{0,112},{1,113},{2,114},{3,115},{4,116},{5,117},{6,118},{7,119},{8... | collective-permute-start | bytes 786440 | tf_op jit(solution)/shard_map/ppermute | solution.py:247
  7.2 21.6 %collective-permute-start.5 = (bf16[1024,128]{1,0:T(8,128)(2,1)}, bf16[1024,128]{1,0:T(8,128)(2,1)S(1)}, u32[]{:S(2)}, u32[]{:S(2)}) collective-permute-start(bf16[1024,128]{1,0:T(8,128)(2,1)} %get-tuple-element.26), channel_id=1, source_target_pairs={{0,96},{16,112},{1,97},{17,113},{2,98},{18,114},{3,99},{19,115},{4... | collective-permute-start | bytes 786440 | tf_op jit(solution)/shard_map/ppermute | solution.py:247
  8.5 19.5 %collective-permute-start.4 = (bf16[1024,128]{1,0:T(8,128)(2,1)}, bf16[1024,128]{1,0:T(8,128)(2,1)S(1)}, u32[]{:S(2)}, u32[]{:S(2)}) collective-permute-start(bf16[1024,128]{1,0:T(8,128)(2,1)} %get-tuple-element.26), channel_id=1, source_target_pairs={{0,80},{16,96},{32,112},{1,81},{17,97},{33,113},{2,82},{18,98},{34... | collective-permute-start | bytes 786440 | tf_op jit(solution)/shard_map/ppermute | solution.py:247
  14.0 12.5 %collective-permute-start.2 = (bf16[1024,128]{1,0:T(8,128)(2,1)}, bf16[1024,128]{1,0:T(8,128)(2,1)S(1)}, u32[]{:S(2)}, u32[]{:S(2)}) collective-permute-start(bf16[1024,128]{1,0:T(8,128)(2,1)} %get-tuple-element.26), channel_id=1, source_target_pairs={{0,48},{16,64},{32,80},{48,96},{64,112},{1,49},{17,65},{33,81},{49... | collective-permute-start | bytes 786440 | tf_op jit(solution)/shard_map/ppermute | solution.py:247
  17.3 10.0 %collective-permute-start.3 = (bf16[1024,128]{1,0:T(8,128)(2,1)}, bf16[1024,128]{1,0:T(8,128)(2,1)S(1)}, u32[]{:S(2)}, u32[]{:S(2)}) collective-permute-start(bf16[1024,128]{1,0:T(8,128)(2,1)} %get-tuple-element.26), channel_id=1, source_target_pairs={{0,64},{16,80},{32,96},{48,112},{1,65},{17,81},{33,97},{49,113},{2... | collective-permute-start | bytes 786440 | tf_op jit(solution)/shard_map/ppermute | solution.py:247
  30.2 17.5 %collective-permute-start.7 = (bf16[7,1024,128]{2,1,0:T(8,128)(2,1)}, bf16[7,1024,128]{2,1,0:T(8,128)(2,1)}, u32[]{:S(2)}, u32[]{:S(2)}) collective-permute-start(bf16[7,1024,128]{2,1,0:T(8,128)(2,1)} %bitcast_dynamic-update-slice_fusion.mine_ref), channel_id=1, source_target_pairs={{0,1},{1,0},{2,3},{3,2},{4,5},{5,4},{6,7},{7,6},{8,9},{9,8},{10,11... | collective-permute-start | bytes 5505032 | tf_op jit(solution)/shard_map/ppermute | solution.py:250
  47.6 58.6 %collective-permute-start.9 = (bf16[512,3072]{1,0:T(8,128)(2,1)}, bf16[512,3072]{1,0:T(8,128)(2,1)S(1)}, u32[]{:S(2)}, u32[]{:S(2)}) collective-permute-start(bf16[512,3072]{1,0:T(8,128)(2,1)} %constant_dynamic-slice_fusion), channel_id=1, source_target_pairs={{0,1},{1,0},{2,3},{3,2},{4,5},{5,4},{6,7},{7,6},{8,9},{9,8},{10,11... | collective-permute-start | bytes 9437192 | tf_op jit(solution)/shard_map/ppermute | solution.py:252
  60.4 39.9 %collective-permute-start.8 = (bf16[256,512]{1,0:T(8,128)(2,1)}, bf16[256,512]{1,0:T(8,128)(2,1)S(1)}, u32[]{:S(2)}, u32[]{:S(2)}) collective-permute-start(bf16[256,512]{1,0:T(8,128)(2,1)} %attend.4.a), channel_id=1, source_target_pairs={{0,1},{1,0},{2,3},{3,2},{4,5},{5,4},{6,7},{7,6},{8,9},{9,8},{10,11... | collective-permute-start | bytes 786440 | tf_op jit(solution)/shard_map/ppermute | solution.py:259
  73.8 27.3 %collective-permute-start.14 = (bf16[256,512]{1,0:T(8,128)(2,1)}, bf16[256,512]{1,0:T(8,128)(2,1)}, u32[]{:S(2)}, u32[]{:S(2)}) collective-permute-start(bf16[256,512]{1,0:T(8,128)(2,1)} %attend.5.a), channel_id=1, source_target_pairs={{0,1},{1,0},{2,3},{3,2},{4,5},{5,4},{6,7},{7,6},{8,9},{9,8},{10,11... | collective-permute-start | bytes 786440 | tf_op jit(solution)/shard_map/ppermute | solution.py:259
  86.9 15.9 %collective-permute-start.19 = (bf16[256,512]{1,0:T(8,128)(2,1)}, bf16[256,512]{1,0:T(8,128)(2,1)}, u32[]{:S(2)}, u32[]{:S(2)}) collective-permute-start(bf16[256,512]{1,0:T(8,128)(2,1)} %attend.6.a), channel_id=1, source_target_pairs={{0,1},{1,0},{2,3},{3,2},{4,5},{5,4},{6,7},{7,6},{8,9},{9,8},{10,11... | collective-permute-start | bytes 786440 | tf_op jit(solution)/shard_map/ppermute | solution.py:259
  100.2 4.3 %collective-permute-start.24 = (bf16[256,512]{1,0:T(8,128)(2,1)}, bf16[256,512]{1,0:T(8,128)(2,1)}, u32[]{:S(2)}, u32[]{:S(2)}) collective-permute-start(bf16[256,512]{1,0:T(8,128)(2,1)} %attend.7.a), channel_id=1, source_target_pairs={{0,1},{1,0},{2,3},{3,2},{4,5},{5,4},{6,7},{7,6},{8,9},{9,8},{10,11... | collective-permute-start | bytes 786440 | tf_op jit(solution)/shard_map/ppermute | solution.py:259
  106.2 1.6 copy-start
  115.1 29.3 %collective-permute-start.25 = (bf16[64,3072]{1,0:T(8,128)(2,1)}, bf16[64,3072]{1,0:T(8,128)(2,1)S(1)}, u32[]{:S(2)}, u32[]{:S(2)}) collective-permute-start(bf16[64,3072]{1,0:T(8,128)(2,1)} %get-tuple-element.40), channel_id=1, source_target_pairs={{0,4},{1,5},{2,6},{3,7},{4,8},{5,9},{6,10},{7,11},{8,12},{9,13},{1... | collective-permute-start | bytes 1179656 | tf_op jit(solution)/shard_map/ppermute | solution.py:262
  116.4 28.3 %collective-permute-start.26 = (bf16[64,3072]{1,0:T(8,128)(2,1)}, bf16[64,3072]{1,0:T(8,128)(2,1)S(1)}, u32[]{:S(2)}, u32[]{:S(2)}) collective-permute-start(bf16[64,3072]{1,0:T(8,128)(2,1)} %get-tuple-element.41), channel_id=1, source_target_pairs={{0,8},{1,9},{2,10},{3,11},{4,12},{5,13},{6,14},{7,15},{8,0},{9,1},... | collective-permute-start | bytes 1179656 | tf_op jit(solution)/shard_map/ppermute | solution.py:262
  118.2 28.0 %collective-permute-start.27 = (bf16[64,3072]{1,0:T(8,128)(2,1)}, bf16[64,3072]{1,0:T(8,128)(2,1)S(1)}, u32[]{:S(2)}, u32[]{:S(2)}) collective-permute-start(bf16[64,3072]{1,0:T(8,128)(2,1)} %get-tuple-element.42), channel_id=1, source_target_pairs={{0,12},{1,13},{2,14},{3,15},{4,0},{5,1},{6,2},{7,3},{8,4},{9,5},{1... | collective-permute-start | bytes 1179656 | tf_op jit(solution)/shard_map/ppermute | solution.py:262
  126.6 21.7 %collective-permute-start.20 = (bf16[64,3072]{1,0:T(8,128)(2,1)}, bf16[64,3072]{1,0:T(8,128)(2,1)S(1)}, u32[]{:S(2)}, u32[]{:S(2)}) collective-permute-start(bf16[64,3072]{1,0:T(8,128)(2,1)} %get-tuple-element.36), channel_id=1, source_target_pairs={{0,4},{1,5},{2,6},{3,7},{4,8},{5,9},{6,10},{7,11},{8,12},{9,13},{1... | collective-permute-start | bytes 1179656 | tf_op jit(solution)/shard_map/ppermute | solution.py:262
  127.1 21.3 %collective-permute-start.21 = (bf16[64,3072]{1,0:T(8,128)(2,1)}, bf16[64,3072]{1,0:T(8,128)(2,1)S(1)}, u32[]{:S(2)}, u32[]{:S(2)}) collective-permute-start(bf16[64,3072]{1,0:T(8,128)(2,1)} %get-tuple-element.37), channel_id=1, source_target_pairs={{0,8},{1,9},{2,10},{3,11},{4,12},{5,13},{6,14},{7,15},{8,0},{9,1},... | collective-permute-start | bytes 1179656 | tf_op jit(solution)/shard_map/ppermute | solution.py:262
  136.8 7.6 %copy-start.11 = (bf16[64,3072]{1,0:T(8,128)(2,1)S(1)}, bf16[64,3072]{1,0:T(8,128)(2,1)}, u32[]{:S(2)}) copy-start(bf16[64,3072]{1,0:T(8,128)(2,1)} %get-tuple-element.38) | copy-start | bytes 1179652
  136.8 7.9 %copy-start.10 = (bf16[64,3072]{1,0:T(8,128)(2,1)S(1)}, bf16[64,3072]{1,0:T(8,128)(2,1)}, u32[]{:S(2)}) copy-start(bf16[64,3072]{1,0:T(8,128)(2,1)} %get-tuple-element.32) | copy-start | bytes 1179652
  136.8 9.3 %copy-start.9 = (bf16[64,3072]{1,0:T(8,128)(2,1)S(1)}, bf16[64,3072]{1,0:T(8,128)(2,1)}, u32[]{:S(2)}) copy-start(bf16[64,3072]{1,0:T(8,128)(2,1)} %get-tuple-element.33) | copy-start | bytes 1179652
  136.8 11.1 %copy-start.4 = (bf16[64,3072]{1,0:T(8,128)(2,1)S(1)}, bf16[64,3072]{1,0:T(8,128)(2,1)}, u32[]{:S(2)}) copy-start(bf16[64,3072]{1,0:T(8,128)(2,1)} %get-tuple-element.39) | copy-start | bytes 1179652
  144.4 3.9 %copy-start.8 = (bf16[64,3072]{1,0:T(8,128)(2,1)S(1)}, bf16[64,3072]{1,0:T(8,128)(2,1)}, u32[]{:S(2)}) copy-start(bf16[64,3072]{1,0:T(8,128)(2,1)} %get-tuple-element.34) | copy-start | bytes 1179652
  144.4 4.0 %copy-start.7 = (bf16[64,3072]{1,0:T(8,128)(2,1)S(1)}, bf16[64,3072]{1,0:T(8,128)(2,1)}, u32[]{:S(2)}) copy-start(bf16[64,3072]{1,0:T(8,128)(2,1)} %get-tuple-element.28) | copy-start | bytes 1179652
  144.4 9.6 %copy-start.6 = (bf16[64,3072]{1,0:T(8,128)(2,1)S(1)}, bf16[64,3072]{1,0:T(8,128)(2,1)}, u32[]{:S(2)}) copy-start(bf16[64,3072]{1,0:T(8,128)(2,1)} %get-tuple-element.29) | copy-start | bytes 1179652
  144.4 11.7 %copy-start.3 = (bf16[64,3072]{1,0:T(8,128)(2,1)S(1)}, bf16[64,3072]{1,0:T(8,128)(2,1)}, u32[]{:S(2)}) copy-start(bf16[64,3072]{1,0:T(8,128)(2,1)} %get-tuple-element.35) | copy-start | bytes 1179652
  144.4 9.5 %collective-permute-start.22 = (bf16[64,3072]{1,0:T(8,128)(2,1)S(1)}, bf16[64,3072]{1,0:T(8,128)(2,1)S(1)}, u32[]{:S(2)}, u32[]{:S(2)}) collective-permute-start(bf16[64,3072]{1,0:T(8,128)(2,1)S(1)} %copy-done.11), channel_id=1, source_target_pairs={{0,12},{1,13},{2,14},{3,15},{4,0},{5,1},{6,2},{7,3},{8,4},{9,5},{1... | collective-permute-start | bytes 1179656 | tf_op jit(solution)/shard_map/ppermute | solution.py:262
  144.7 14.9 %collective-permute-start.15 = (bf16[64,3072]{1,0:T(8,128)(2,1)S(1)}, bf16[64,3072]{1,0:T(8,128)(2,1)S(1)}, u32[]{:S(2)}, u32[]{:S(2)}) collective-permute-start(bf16[64,3072]{1,0:T(8,128)(2,1)S(1)} %copy-done.10), channel_id=1, source_target_pairs={{0,4},{1,5},{2,6},{3,7},{4,8},{5,9},{6,10},{7,11},{8,12},{9,13},{1... | collective-permute-start | bytes 1179656 | tf_op jit(solution)/shard_map/ppermute | solution.py:262
  146.2 17.3 %collective-permute-start.16 = (bf16[64,3072]{1,0:T(8,128)(2,1)S(1)}, bf16[64,3072]{1,0:T(8,128)(2,1)S(1)}, u32[]{:S(2)}, u32[]{:S(2)}) collective-permute-start(bf16[64,3072]{1,0:T(8,128)(2,1)S(1)} %copy-done.9), channel_id=1, source_target_pairs={{0,8},{1,9},{2,10},{3,11},{4,12},{5,13},{6,14},{7,15},{8,0},{9,1},... | collective-permute-start | bytes 1179656 | tf_op jit(solution)/shard_map/ppermute | solution.py:262
  148.2 11.4 %copy-start.5 = (bf16[64,3072]{1,0:T(8,128)(2,1)S(1)}, bf16[64,3072]{1,0:T(8,128)(2,1)}, u32[]{:S(2)}) copy-start(bf16[64,3072]{1,0:T(8,128)(2,1)} %get-tuple-element.30) | copy-start | bytes 1179652
  148.2 23.9 %copy-start.2 = (bf16[64,3072]{1,0:T(8,128)(2,1)S(1)}, bf16[64,3072]{1,0:T(8,128)(2,1)}, u32[]{:S(2)}) copy-start(bf16[64,3072]{1,0:T(8,128)(2,1)} %get-tuple-element.31) | copy-start | bytes 1179652
  148.2 22.5 %collective-permute-start.17 = (bf16[64,3072]{1,0:T(8,128)(2,1)S(1)}, bf16[64,3072]{1,0:T(8,128)(2,1)S(1)}, u32[]{:S(2)}, u32[]{:S(2)}) collective-permute-start(bf16[64,3072]{1,0:T(8,128)(2,1)S(1)} %copy-done.8), channel_id=1, source_target_pairs={{0,12},{1,13},{2,14},{3,15},{4,0},{5,1},{6,2},{7,3},{8,4},{9,5},{1... | collective-permute-start | bytes 1179656 | tf_op jit(solution)/shard_map/ppermute | solution.py:262
  148.4 28.0 %collective-permute-start.10 = (bf16[64,3072]{1,0:T(8,128)(2,1)S(1)}, bf16[64,3072]{1,0:T(8,128)(2,1)S(1)}, u32[]{:S(2)}, u32[]{:S(2)}) collective-permute-start(bf16[64,3072]{1,0:T(8,128)(2,1)S(1)} %copy-done.7), channel_id=1, source_target_pairs={{0,4},{1,5},{2,6},{3,7},{4,8},{5,9},{6,10},{7,11},{8,12},{9,13},{1... | collective-permute-start | bytes 1179656 | tf_op jit(solution)/shard_map/ppermute | solution.py:262
  153.9 25.3 %collective-permute-start.11 = (bf16[64,3072]{1,0:T(8,128)(2,1)S(1)}, bf16[64,3072]{1,0:T(8,128)(2,1)S(1)}, u32[]{:S(2)}, u32[]{:S(2)}) collective-permute-start(bf16[64,3072]{1,0:T(8,128)(2,1)S(1)} %copy-done.6), channel_id=1, source_target_pairs={{0,8},{1,9},{2,10},{3,11},{4,12},{5,13},{6,14},{7,15},{8,0},{9,1},... | collective-permute-start | bytes 1179656 | tf_op jit(solution)/shard_map/ppermute | solution.py:262
  156.3 30.8 %copy-start.1 = (bf16[64,3072]{1,0:T(8,128)(2,1)S(1)}, bf16[64,3072]{1,0:T(8,128)(2,1)}, u32[]{:S(2)}) copy-start(bf16[64,3072]{1,0:T(8,128)(2,1)} %get-tuple-element.27) | copy-start | bytes 1179652
  159.6 27.5 %collective-permute-start.12 = (bf16[64,3072]{1,0:T(8,128)(2,1)S(1)}, bf16[64,3072]{1,0:T(8,128)(2,1)S(1)}, u32[]{:S(2)}, u32[]{:S(2)}) collective-permute-start(bf16[64,3072]{1,0:T(8,128)(2,1)S(1)} %copy-done.5), channel_id=1, source_target_pairs={{0,12},{1,13},{2,14},{3,15},{4,0},{5,1},{6,2},{7,3},{8,4},{9,5},{1... | collective-permute-start | bytes 1179656 | tf_op jit(solution)/shard_map/ppermute | solution.py:262
  163.5 25.3 %collective-permute-start.28 = (bf16[32,3072]{1,0:T(8,128)(2,1)S(1)}, bf16[32,3072]{1,0:T(8,128)(2,1)S(1)}, u32[]{:S(2)}, u32[]{:S(2)}) collective-permute-start(bf16[32,3072]{1,0:T(8,128)(2,1)S(1)} %slice.116), channel_id=1, source_target_pairs={{0,2},{1,3},{2,0},{3,1},{4,6},{5,7},{6,4},{7,5},{8,10},{9,11},{10,... | collective-permute-start | bytes 589832 | tf_op jit(solution)/shard_map/ppermute | solution.py:267
  170.7 18.1 %collective-permute-start.23 = (bf16[32,3072]{1,0:T(8,128)(2,1)S(1)}, bf16[32,3072]{1,0:T(8,128)(2,1)S(1)}, u32[]{:S(2)}, u32[]{:S(2)}) collective-permute-start(bf16[32,3072]{1,0:T(8,128)(2,1)S(1)} %slice.117), channel_id=1, source_target_pairs={{0,2},{1,3},{2,0},{3,1},{4,6},{5,7},{6,4},{7,5},{8,10},{9,11},{10,... | collective-permute-start | bytes 589832 | tf_op jit(solution)/shard_map/ppermute | solution.py:267
  176.4 12.5 %collective-permute-start.18 = (bf16[32,3072]{1,0:T(8,128)(2,1)S(1)}, bf16[32,3072]{1,0:T(8,128)(2,1)S(1)}, u32[]{:S(2)}, u32[]{:S(2)}) collective-permute-start(bf16[32,3072]{1,0:T(8,128)(2,1)S(1)} %slice.118), channel_id=1, source_target_pairs={{0,2},{1,3},{2,0},{3,1},{4,6},{5,7},{6,4},{7,5},{8,10},{9,11},{10,... | collective-permute-start | bytes 589832 | tf_op jit(solution)/shard_map/ppermute | solution.py:267
  187.4 5.7 %collective-permute-start.13 = (bf16[32,3072]{1,0:T(8,128)(2,1)S(1)}, bf16[32,3072]{1,0:T(8,128)(2,1)S(1)}, u32[]{:S(2)}, u32[]{:S(2)}) collective-permute-start(bf16[32,3072]{1,0:T(8,128)(2,1)S(1)} %slice.119), channel_id=1, source_target_pairs={{0,2},{1,3},{2,0},{3,1},{4,6},{5,7},{6,4},{7,5},{8,10},{9,11},{10,... | collective-permute-start | bytes 589832 | tf_op jit(solution)/shard_map/ppermute | solution.py:267
  193.2 4.2 %collective-permute-start.29 = (bf16[64,3072]{1,0:T(8,128)(2,1)S(1)}, bf16[64,3072]{1,0:T(8,128)(2,1)S(1)}, u32[]{:S(2)}, u32[]{:S(2)}) collective-permute-start(bf16[64,3072]{1,0:T(8,128)(2,1)S(1)} %pad_maximum_fusion.2), channel_id=1, source_target_pairs={{0,1},{1,0},{2,3},{3,2},{4,5},{5,4},{6,7},{7,6},{8,9},{9,8},{10,11... | collective-permute-start | bytes 1179656 | tf_op jit(solution)/shard_map/ppermute | solution.py:272

commit v2 on v1

v2 whole, which is shorter than its diff:
```python
import functools

import jax
import jax.numpy as jnp
from jax import lax
from jax.experimental import pallas as pl
from jax.experimental.pallas import tpu as pltpu
from jax.sharding import PartitionSpec as P

KV_HEADS = 8
DH = 128
LOG2E = 1.4426950408889634
NEG = -1e30
LIMIT = 60.0
CHUNKS = 4
BF = jnp.bfloat16
F32 = jnp.float32
VMEM_LIMIT = 56 << 20
PARAMS = pltpu.CompilerParams(vmem_limit_bytes=VMEM_LIMIT)


def after(x, *deps):
    return lax.optimization_barrier((x, *deps))[0]


def prep_kernel(info, k_ref, v_ref, kv_ref):
    rows = k_ref.shape[0]
    kv_ref[0:rows, :] = k_ref[...]
    for t in range(rows // DH):
        kv_ref[rows + t * DH : rows + (t + 1) * DH, :] = v_ref[t * DH : (t + 1) * DH, :].T


def prep(info, keys, values):
    rows = keys.shape[0]
    col = pl.BlockSpec((rows, DH), lambda i, info: (0, info[1]))
    return pl.pallas_call(
        prep_kernel,
        grid_spec=pltpu.PrefetchScalarGridSpec(
            num_scalar_prefetch=1,
            grid=(1,),
            in_specs=[col, col],
            out_specs=pl.BlockSpec((2 * rows, DH), lambda i, info: (0, 0)),
        ),
        out_shape=jax.ShapeDtypeStruct((2 * rows, DH), BF),
        name="prep",
        compiler_params=PARAMS,
    )(info, keys, values)


def keys_of(kv):
    k = kv[0 : kv.shape[0] // 2, :]
    return jnp.concatenate([k, k], axis=1)


def values_of(kv):
    rows = kv.shape[0] // 2
    tiles = [kv[rows + t * DH : rows + (t + 1) * DH, :] for t in range(rows // DH)]
    return jnp.concatenate([jnp.concatenate(tiles, axis=1), jnp.ones((16, rows), BF)], axis=0)


def diagonal_kernel(groups, q_ref, kv_ref, qt_ref, acc_ref, m_ref):
    chunk = pl.program_id(0)
    _, _, sub, width = q_ref.shape
    rows = kv_ref.shape[0] // 2
    heads, qb = width // DH, groups * sub
    half = heads * qb // 2
    for h in range(heads):
        qh = q_ref[:, 0, :, h * DH : (h + 1) * DH].reshape(qb, DH).astype(F32) * (DH**-0.5 * LOG2E)
        high = qh.astype(BF)
        low = (qh - high.astype(F32)).astype(BF)
        qt_ref[0, 0:DH, h * qb : (h + 1) * qb] = high.T
        qt_ref[0, DH : 2 * DH, h * qb : (h + 1) * qb] = low.T
    kk, vt = keys_of(kv_ref[...]), values_of(kv_ref[...])
    col = lax.broadcasted_iota(jnp.int32, (rows, half), 1) % qb
    pos = (col // sub) * (rows // groups) + chunk * sub + col % sub
    allowed = lax.broadcasted_iota(jnp.int32, (rows, half), 0) <= pos
    for c0 in (0, half):
        s = jnp.dot(kk, qt_ref[0, :, c0 : c0 + half], preferred_element_type=F32)
        s = jnp.where(allowed, s, NEG)
        m = jnp.max(s, axis=0, keepdims=True)
        m_ref[0, :, c0 : c0 + half] = jnp.broadcast_to(m, (8, half))
        acc_ref[0, :, c0 : c0 + half] = jnp.dot(vt, jnp.exp2(s - m).astype(BF), preferred_element_type=F32)


def diagonal(q4, kv):
    groups, chunks, sub, width = q4.shape
    cols = groups * sub * width // DH
    one = lambda i: (i, 0, 0)
    return pl.pallas_call(
        functools.partial(diagonal_kernel, groups),
        grid=(chunks,),
        in_specs=[
            pl.BlockSpec((groups, 1, sub, width), lambda i: (0, i, 0, 0)),
            pl.BlockSpec(kv.shape, lambda i: (0, 0)),
        ],
        out_specs=[
            pl.BlockSpec((1, 2 * DH, cols), one),
            pl.BlockSpec((1, DH + 16, cols), one),
            pl.BlockSpec((1, 8, cols), one),
        ],
        out_shape=[
            jax.ShapeDtypeStruct((chunks, 2 * DH, cols), BF),
            jax.ShapeDtypeStruct((chunks, DH + 16, cols), F32),
            jax.ShapeDtypeStruct((chunks, 8, cols), F32),
        ],
        name="diagonal",
        cost_estimate=pl.CostEstimate(
            flops=chunks * cols * kv.shape[0] * 2 * DH, bytes_accessed=8 << 20, transcendentals=0
        ),
        compiler_params=PARAMS,
    )(q4, kv)


def attend_kernel(first, count, chunk, final, groups, n_y, info, *refs):
    ops = (count + 1) // 2
    qt_hbm, acc_hbm, m_hbm = refs[:3]
    mine, other = refs[3 : 3 + ops], refs[3 + ops : 3 + 2 * ops]
    refs = refs[3 + 2 * ops :]
    outs, (kv_buf, qt_ref, acc_ref, m_ref, mx_ref, sems) = refs[:-6], refs[-6:]
    place, core = info[0], info[2]
    rows = kv_buf.shape[1] // 2
    cols = qt_ref.shape[1]
    half = cols // 2
    todo = jnp.clip(place - first, 0, count)
    loads = [
        pltpu.make_async_copy(qt_hbm, qt_ref, sems.at[count]),
        pltpu.make_async_copy(acc_hbm, acc_ref.at[0], sems.at[count + 1]),
        pltpu.make_async_copy(m_hbm, m_ref, sems.at[count + 2]),
    ]
    for load in loads:
        load.start()
    for i in range(count):
        @pl.when(jnp.logical_and(i < todo, core == i % 2))
        def _():
            pltpu.make_async_copy(mine[i // 2], kv_buf.at[i], sems.at[i]).start()

        @pl.when(jnp.logical_and(i < todo, core != i % 2))
        def _():
            pltpu.make_async_copy(other[i // 2], kv_buf.at[i], sems.at[i]).start()

    for load in loads:
        load.wait()

    def scores(kk, c0):
        return jnp.dot(kk, qt_ref[:, c0 : c0 + half], preferred_element_type=F32)

    def body(i, _):
        pltpu.make_async_copy(mine[0], kv_buf.at[i], sems.at[i]).wait()
        old, new = i % 2, (i + 1) % 2
        kk, vt = keys_of(kv_buf.at[i]), values_of(kv_buf.at[i])
        for c0 in (0, half):
            s = scores(kk, c0)
            mx_ref[:, c0 : c0 + half] = jnp.max(s.reshape(rows // 8, 8, half), axis=0)
            p = jnp.exp2(s - m_ref[0:1, c0 : c0 + half]).astype(BF)
            acc_ref[new, :, c0 : c0 + half] = acc_ref[old, :, c0 : c0 + half] + jnp.dot(
                vt, p, preferred_element_type=F32
            )
        over = jnp.max(mx_ref[...] - m_ref[...])

        @pl.when(over > LIMIT)
        def _():
            for c0 in (0, half):
                m = m_ref[0:1, c0 : c0 + half]
                top = jnp.maximum(m, jnp.max(mx_ref[:, c0 : c0 + half], axis=0, keepdims=True))
                p = jnp.exp2(scores(kk, c0) - top).astype(BF)
                acc_ref[new, :, c0 : c0 + half] = acc_ref[old, :, c0 : c0 + half] * jnp.exp2(
                    m - top
                ) + jnp.dot(vt, p, preferred_element_type=F32)
                m_ref[:, c0 : c0 + half] = jnp.broadcast_to(top, (8, half))

        return 0

    lax.fori_loop(0, todo, body, 0)
    last = todo % 2
    if not final:
        outs[0][0] = acc_ref[last]
        outs[1][0] = m_ref[...]
        return
    (o_ref,) = outs
    qb = o_ref.shape[0]
    sub = qb // groups
    for h in range(o_ref.shape[1] // DH):
        o = acc_ref[last, :, h * qb : (h + 1) * qb]
        o = (o[0:DH] / o[DH : DH + 1]).T.astype(BF)
        for g in range(groups):
            ry = (g // 4 + n_y - info[3]) % n_y
            rz = (g // 2 % 2) ^ info[4]
            dst = (ry * 2 + rz) if chunk % 2 == 0 else (rz * n_y + ry)
            dst = pl.multiple_of((dst * 2 + g % 2) * sub, sub)
            o_ref[pl.ds(dst, sub), h * DH : (h + 1) * DH] = o[g * sub : (g + 1) * sub, :]


def attend(info, qt, acc, m, mine, other, first, count, chunk, slot, final, groups, n_y, width):
    cols = qt.shape[2]
    qb = cols // (width // DH)
    rows2 = mine[0].shape[0]
    any_space = pl.BlockSpec(memory_space=pl.ANY)
    if final:
        out_specs = pl.BlockSpec((qb, width), lambda i, info: (0, 0))
        out_shape = jax.ShapeDtypeStruct((qb, width), BF)
    else:
        out_specs = [
            pl.BlockSpec((1, DH + 16, cols), lambda i, info: (0, 0, 0)),
            pl.BlockSpec((1, 8, cols), lambda i, info: (0, 0, 0)),
        ]
        out_shape = [
            jax.ShapeDtypeStruct((1, DH + 16, cols), F32),
            jax.ShapeDtypeStruct((1, 8, cols), F32),
        ]

    def body(info, qt_ref, acc_ref, m_ref, *refs):
        attend_kernel(
            first, count, chunk, final, groups, n_y, info,
            qt_ref.at[chunk], acc_ref.at[slot], m_ref.at[slot], *refs,
        )

    return pl.pallas_call(
        body,
        grid_spec=pltpu.PrefetchScalarGridSpec(
            num_scalar_prefetch=1,
            grid=(1,),
            in_specs=[any_space] * (3 + 2 * len(mine)),
            out_specs=out_specs,
            scratch_shapes=[
                pltpu.VMEM((count, rows2, DH), BF),
                pltpu.VMEM((2 * DH, cols), BF),
                pltpu.VMEM((2, DH + 16, cols), F32),
                pltpu.VMEM((8, cols), F32),
                pltpu.VMEM((8, cols), F32),
                pltpu.SemaphoreType.DMA((count + 3,)),
            ],
        ),
        out_shape=out_shape,
        name="attend",
        cost_estimate=pl.CostEstimate(
            flops=4 * cols * rows2 * count * DH, bytes_accessed=4 << 20, transcendentals=0
        ),
        compiler_params=PARAMS,
    )(info, qt, acc, m, *mine, *other)


def project(info, mine, other, w, w_other, parts, tile):
    rows, width = mine.shape
    n = w.shape[1] // 2
    steps = n // tile

    def body(info, a, b, wa, wb, *outs):
        s = jnp.dot(a[...], wa[...], preferred_element_type=F32) + jnp.dot(
            b[...], wb[...], preferred_element_type=F32
        )
        part = s.shape[0] // len(outs)
        for i, o in enumerate(outs):
            o[...] = s[i * part : (i + 1) * part].astype(BF)

    whole = pl.BlockSpec((rows, width), lambda i, info: (0, 0))
    weights = pl.BlockSpec((width, tile), lambda i, info: (0, info[2] * steps + i))
    return pl.pallas_call(
        body,
        grid_spec=pltpu.PrefetchScalarGridSpec(
            num_scalar_prefetch=1,
            grid=(steps,),
            in_specs=[whole, whole, weights, weights],
            out_specs=[pl.BlockSpec((rows // parts, tile), lambda i, info: (0, i))] * parts,
        ),
        out_shape=[jax.ShapeDtypeStruct((rows // parts, n), BF)] * parts,
        name="project",
        cost_estimate=pl.CostEstimate(
            flops=4 * rows * width * n, bytes_accessed=4 * width * n + 4 * rows * n, transcendentals=0
        ),
        compiler_params=PARAMS,
    )(info, mine, other, w, w_other)


def add(*terms):
    total = terms[0].astype(F32)
    for t in terms[1:]:
        total = total + t.astype(F32)
    return total.astype(BF)


def local(queries, keys, values, w_out):
    n_seq, n_head = lax.axis_size("seq"), lax.axis_size("head")
    rows, width = queries.shape
    cols = w_out.shape[1]
    place = lax.axis_index("seq")
    head = lax.axis_index("head")
    core, y, z = head % 2, head // 4, head // 2 % 2
    n_y = n_head // 4
    info = jnp.stack([place, head * KV_HEADS // n_head, core, y, z]).astype(jnp.int32)

    def to(f):
        return [(h, f(h // 4, h // 2 % 2, h % 2)) for h in range(n_head)]

    def at(y, z, c):
        return (y % n_y) * 4 + z * 2 + c

    swap_core = to(lambda y, z, c: at(y, z, 1 - c))
    swap_z = to(lambda y, z, c: at(y, 1 - z, c))
    by_y = {d: to(lambda y, z, c, d=d: at(y + d, z, c)) for d in range(1, n_y)}

    def over_head(x, pairs):
        return lax.ppermute(x, "head", pairs)

    kv = prep(info, keys, values)
    mine = []
    for op in range(n_seq // 2):
        pairs = []
        for s in range(n_seq):
            for h in range(n_head):
                d = 2 * op + 1 + h % 2
                if s + d < n_seq:
                    pairs.append((s * n_head + h, (s + d) * n_head + h))
        mine.append(lax.ppermute(kv, ("seq", "head"), pairs))
    sub = rows // n_head // CHUNKS
    q4 = queries.reshape(n_head, CHUNKS, sub, width)
    qt, acc, m = diagonal(q4, kv)
    near = n_seq // 4
    other = [over_head(x, swap_core) for x in mine[:near]]
    w_other = over_head(after(w_out, m), swap_core)

    def run(acc, m, slot, ops, chunk, final, *deps):
        first = 2 * ops[0]
        count = min(2 * len(ops), n_seq - 1 - first)
        return attend(
            after(info, *deps), qt, acc, m, [mine[i] for i in ops], [other[i] for i in ops],
            first, count, chunk, slot, final, n_head, n_y, width,
        )

    ops = list(range(n_seq // 2))
    acc0, m0 = run(acc, m, 0, ops[:near], 0, False)
    other += [over_head(after(x, m0), swap_core) for x in mine[near:]]
    acc1, m1 = run(acc, m, 1, ops[:near], 1, False, acc0)
    out = [None] * CHUNKS
    out[0] = run(acc0, m0, 0, ops[near:], 0, True, acc1)
    far = [None] * CHUNKS
    far[0] = over_head(out[0], swap_core)
    out[1] = run(acc1, m1, 0, ops[near:], 1, True, out[0])
    far[1] = over_head(out[1], swap_core)

    def projected(i, *deps):
        return project(after(info, *deps), out[i], far[i], w_out, w_other, n_y if i % 2 == 0 else 2, cols // 4)

    def first_stage(i, parts):
        if i % 2 == 0:
            return [over_head(parts[d], by_y[d]) for d in range(1, n_y)]
        return [over_head(parts[1], swap_z)]

    def second_stage(i, total):
        if i % 2 == 0:
            return total[: 2 * sub], [over_head(total[2 * sub :], swap_z)]
        got = [over_head(total[d * 2 * sub : (d + 1) * 2 * sub], by_y[d]) for d in range(1, n_y)]
        return total[: 2 * sub], got

    parts0 = projected(0, out[1])
    got0 = first_stage(0, parts0)
    out[2] = run(acc, m, 2, ops, 2, True, parts0[0])
    far[2] = over_head(out[2], swap_core)
    parts1 = projected(1, out[2])
    got1 = first_stage(1, parts1)
    sum0 = add(parts0[0], *got0)
    keep0, back0 = second_stage(0, sum0)
    out[3] = run(acc, m, 3, ops, 3, True, parts1[0], sum0)
    far[3] = over_head(out[3], swap_core)
    parts2 = projected(2, out[3])
    got2 = first_stage(2, parts2)
    sum1 = add(after(parts1[0], parts2[0]), *got1)
    keep1, back1 = second_stage(1, sum1)
    parts3 = projected(3, parts2[0], sum1)
    got3 = first_stage(3, parts3)
    sum2 = add(after(parts2[0], parts3[0]), *got2)
    keep2, back2 = second_stage(2, sum2)
    sum3 = add(parts3[0], *got3)
    keep3, back3 = second_stage(3, sum3)
    pieces = [
        add(k, *b).reshape(2, sub, cols // 2)
        for k, b in ((keep0, back0), (keep1, back1), (keep2, back2), (keep3, back3))
    ]
    done = jnp.concatenate([jnp.where(core == 0, p[0], p[1]) for p in pieces], axis=0)
    away = jnp.concatenate([jnp.where(core == 0, p[1], p[0]) for p in pieces], axis=0)
    back = over_head(away, swap_core)
    left = jnp.where(core == 0, done, back)
    right = jnp.where(core == 0, back, done)
    return jnp.concatenate([left, right], axis=1)


def solution(mesh):
    placed = (P("seq", "head"), P("seq", None), P("seq", None), P("head", None))
    return jax.shard_map(
        local, mesh=mesh, in_specs=placed, out_specs=P(("seq", "head"), None), check_vma=False
    )
```

time: 200 us -> 193 us (0.965)
  the two profiles are of different devices: /device:TPU:79 before, /device:TPU:71 now
where the time goes in v2:
time: 193 us
  Pallas kernels  85.5 us (44%)
  waiting for transfers between devices  62.5 us (32%)
  starting transfers between devices  36.8 us (19%)
  local copies, waits for them, and re-layouts  5.25 us (3%)
  other arithmetic  2.24 us (1%)
    pallas_call x6, Pallas kernels, attend(): pl.pallas_call(body, grid_spec=pltpu.PrefetchScalarGridSpec(num_scalar_pr...  50.5 us
    ppermute x26, waiting for transfers between devices, over_head(): return lax.ppermute(x, 'head', pairs)  39.5 us
    ppermute x26, starting transfers between devices, over_head(): return lax.ppermute(x, 'head', pairs)  32.3 us
    ppermute x4, waiting for transfers between devices, local(): mine.append(lax.ppermute(kv, ('seq', 'head'), pairs))  23 us
    pallas_call x4, Pallas kernels, project(): pl.pallas_call(body, grid_spec=pltpu.PrefetchScalarGridSpec(num_scalar_pr...  22.3 us
    pallas_call x1, Pallas kernels, diagonal(): pl.pallas_call(functools.partial(diagonal_kernel, groups), grid=(chunks,)...  10.1 us
    ppermute x4, starting transfers between devices, local(): mine.append(lax.ppermute(kv, ('seq', 'head'), pairs))  4.55 us
    unnamed x36, local copies, waits for them, and re-layouts  4.51 us
  transfers between devices with their start and end apart: 30, of which 12 were waited for; matrix products, arithmetic and copies ran while one was open for 0% of the time, Pallas kernels for 38%

profile of v2, /device:TPU:71, one launch (start us, length us, event | category | flops | bytes accessed | tf_op | source)
XLA Modules:
  0.0 192.8 jit_solution(16259455839955015603)
XLA Ops:
  0.6 2.6 %prep.1.kv_ref = bf16[2048,128]{1,0:T(8,128)(2,1)} custom-call(s32[5]{0:T(128)} %stack.23.info, bf16[1024,1024]{1,0:T(8,128)(2,1)} %k_ref.1, bf16[1024,1024]{1,0:T(8,128)(2,1)} %v_ref.1), custom_call_target="tpu_custom_call" | custom-call | tf_op jit(solution)/shard_map/prep/pallas_call | solution.py:36
  3.2 10.1 %diagonal.1 = (bf16[4,256,1024]{2,1,0:T(8,128)(2,1)}, f32[4,144,1024]{2,1,0:T(8,128)}, f32[4,8,1024]{2,1,0:T(8,128)}) custom-call(bf16[16,4,16,512]{3,2,1,0:T(8,128)(2,1)} %bitcast.6, bf16[2048,128]{1,0:T(8,128)(2,1)} %prep.1.kv_ref), custom_call_target="tpu_custom_call" | custom-call | flops 2147483648 | bytes 8388608 | tf_op jit(solution)/shard_map/diagonal/pallas_call | solution.py:89
  13.4 0.7 collective-permute-start.9
  14.0 1.3 collective-permute-start
  15.3 1.3 collective-permute-start.1
  16.6 12.8 %collective-permute-done.refs_0_ = bf16[2048,128]{1,0:T(8,128)(2,1)S(1)} collective-permute-done((bf16[2048,128]{1,0:T(8,128)(2,1)S(1)}, bf16[2048,128]{1,0:T(8,128)(2,1)S(1)}, u32[]{:S(2)}, u32[]{:S(2)}) %collective-permute-start) | collective-permute-done | bytes 524320 | tf_op jit(solution)/shard_map/ppermute | solution.py:313
  29.4 2.8 %collective-permute-start.2 = (bf16[2048,128]{1,0:T(8,128)(2,1)S(1)}, bf16[2048,128]{1,0:T(8,128)(2,1)S(1)}, u32[]{:S(2)}, u32[]{:S(2)}) collective-permute-start(bf16[2048,128]{1,0:T(8,128)(2,1)S(1)} %collective-permute-done.refs_0_), channel_id=1, source_target_pairs={{0,1},{1,0},{2,3},{3,2},{4,5},{5,4},{6,7},{7,6},{8,9},{9,8},{10,11... | collective-permute-start | bytes 1572872 | tf_op jit(solution)/shard_map/ppermute | solution.py:302
  32.3 1.3 collective-permute-start.4
  33.6 0.7 collective-permute-start.5
  35.3 7.5 %attend.6 = (f32[1,144,1024]{2,1,0:T(8,128)}, f32[1,8,1024]{2,1,0:T(8,128)}) custom-call(s32[5]{0:T(128)} %stack.23.info, bf16[4,256,1024]{2,1,0:T(8,128)(2,1)} %get-tuple-element.38.qt_ref, f32[4,144,1024]{2,1,0:T(8,128)} %get-tuple-element.39.acc_ref, f32[4,8,1024]{2,1,0:T(8,128)} %get-tuple-element.40.m_ref, bf16[2048,128]{1,0:T(8,128)(2,1)} %copy-done.10, ...), custom_call_target="tpu_custom_call" | custom-call | flops 4294967296 | bytes 4194304 | tf_op jit(solution)/shard_map/attend/pallas_call | solution.py:217
  42.8 10.2 %collective-permute-done.4.refs_0_.refs_2_ = bf16[2048,128]{1,0:T(8,128)(2,1)S(1)} collective-permute-done((bf16[2048,128]{1,0:T(8,128)(2,1)S(1)}, bf16[2048,128]{1,0:T(8,128)(2,1)S(1)}, u32[]{:S(2)}, u32[]{:S(2)}) %collective-permute-start.4) | collective-permute-done | bytes 524320 | tf_op jit(solution)/shard_map/ppermute | solution.py:313
  53.1 5.7 %collective-permute-start.7 = (bf16[2048,128]{1,0:T(8,128)(2,1)S(1)}, bf16[2048,128]{1,0:T(8,128)(2,1)S(1)}, u32[]{:S(2)}, u32[]{:S(2)}) collective-permute-start(bf16[2048,128]{1,0:T(8,128)(2,1)S(1)} %collective-permute-done.5.refs_1_.refs_3_), channel_id=1, source_target_pairs={{0,1},{1,0},{2,3},{3,2},{4,5},{5,4},{6,7},{7,6},{8,9},{9,8},{10,11... | collective-permute-start | bytes 1572872 | tf_op jit(solution)/shard_map/ppermute | solution.py:302
  58.8 7.5 %attend.7 = (f32[1,144,1024]{2,1,0:T(8,128)}, f32[1,8,1024]{2,1,0:T(8,128)}) custom-call(s32[5]{0:T(128)} %stack.23.info, bf16[4,256,1024]{2,1,0:T(8,128)(2,1)} %get-tuple-element.38.qt_ref, f32[4,144,1024]{2,1,0:T(8,128)} %get-tuple-element.39.acc_ref, f32[4,8,1024]{2,1,0:T(8,128)} %get-tuple-element.40.m_ref, bf16[2048,128]{1,0:T(8,128)(2,1)} %copy-done.10, ...), custom_call_target="tpu_custom_call" | custom-call | flops 4294967296 | bytes 4194304 | tf_op jit(solution)/shard_map/attend/pallas_call | solution.py:217
  66.3 0.8 copy-done.16
  67.1 0.8 copy-done.17
  67.9 6.3 %attend.8.a = bf16[256,512]{1,0:T(8,128)(2,1)} custom-call(s32[5]{0:T(128)} %stack.23.info, bf16[4,256,1024]{2,1,0:T(8,128)(2,1)} %get-tuple-element.38.qt_ref, f32[1,144,1024]{2,1,0:T(8,128)} %get-tuple-element.41.acc_ref, f32[1,8,1024]{2,1,0:T(8,128)} %get-tuple-element.45.m_ref, bf16[2048,128]{1,0:T(8,128)(2,1)} %copy-done.14, ...), custom_call_target="tpu_custom_call" | custom-call | flops 3221225472 | bytes 4194304 | tf_op jit(solution)/shard_map/attend/pallas_call | solution.py:217
  74.2 1.2 collective-permute-start.8
  75.5 6.4 %attend.9.a = bf16[256,512]{1,0:T(8,128)(2,1)} custom-call(s32[5]{0:T(128)} %stack.23.info, bf16[4,256,1024]{2,1,0:T(8,128)(2,1)} %get-tuple-element.38.qt_ref, f32[1,144,1024]{2,1,0:T(8,128)} %get-tuple-element.43.acc_ref, f32[1,8,1024]{2,1,0:T(8,128)} %get-tuple-element.49.m_ref, bf16[2048,128]{1,0:T(8,128)(2,1)} %copy-done.14, ...), custom_call_target="tpu_custom_call" | custom-call | flops 3221225472 | bytes 4194304 | tf_op jit(solution)/shard_map/attend/pallas_call | solution.py:217
  81.9 0.7 copy-done.8
  82.6 5.6 %project.4 = (bf16[64,3072]{1,0:T(8,128)(2,1)}, bf16[64,3072]{1,0:T(8,128)(2,1)}, bf16[64,3072]{1,0:T(8,128)(2,1)}, bf16[64,3072]{1,0:T(8,128)(2,1)}) custom-call(s32[5]{0:T(128)} %stack.23.info, bf16[256,512]{1,0:T(8,128)(2,1)} %attend.8.a, bf16[256,512]{1,0:T(8,128)(2,1)} %copy-done.8, bf16[512,6144]{1,0:T(8,128)(2,1)} %wa.7, ...), custom_call_target="tpu_custom_call" | custom-call | flops 1610612736 | bytes 9437184 | tf_op jit(solution)/shard_map/project/pallas_call | solution.py:257
  88.2 0.6 collective-permute-start.10
  88.8 2.6 %collective-permute-start.11 = (bf16[64,3072]{1,0:T(8,128)(2,1)}, bf16[64,3072]{1,0:T(8,128)(2,1)S(1)}, u32[]{:S(2)}, u32[]{:S(2)}) collective-permute-start(bf16[64,3072]{1,0:T(8,128)(2,1)} %get-tuple-element.54), channel_id=1, source_target_pairs={{0,8},{1,9},{2,10},{3,11},{4,12},{5,13},{6,14},{7,15},{8,0},{9,1},... | collective-permute-start | bytes 1179656 | tf_op jit(solution)/shard_map/ppermute | solution.py:302
  91.5 1.1 collective-permute-start.12
  92.5 12.0 %attend.10.a = bf16[256,512]{1,0:T(8,128)(2,1)} custom-call(s32[5]{0:T(128)} %stack.23.info, bf16[4,256,1024]{2,1,0:T(8,128)(2,1)} %get-tuple-element.38.qt_ref, f32[4,144,1024]{2,1,0:T(8,128)} %get-tuple-element.39.acc_ref, f32[4,8,1024]{2,1,0:T(8,128)} %get-tuple-element.40.m_ref, bf16[2048,128]{1,0:T(8,128)(2,1)} %copy-done.10, ...), custom_call_target="tpu_custom_call" | custom-call | flops 7516192768 | bytes 4194304 | tf_op jit(solution)/shard_map/attend/pallas_call | solution.py:217
  104.7 0.7 copy-done.7
  105.4 5.5 %project.5 = (bf16[128,3072]{1,0:T(8,128)(2,1)}, bf16[128,3072]{1,0:T(8,128)(2,1)}) custom-call(s32[5]{0:T(128)} %stack.23.info, bf16[256,512]{1,0:T(8,128)(2,1)} %attend.9.a, bf16[256,512]{1,0:T(8,128)(2,1)} %copy-done.7, bf16[512,6144]{1,0:T(8,128)(2,1)} %wa.7, bf16[512,6144]{1,0:T(8,128)(2,1)} %collective-permute-done.9.wb), custom_call_target="tpu_custom_call" | custom-call | flops 1610612736 | bytes 9437184 | tf_op jit(solution)/shard_map/project/pallas_call | solution.py:257
  110.9 1.2 collective-permute-start.16
  112.7 10.8 %attend.11.a = bf16[256,512]{1,0:T(8,128)(2,1)} custom-call(s32[5]{0:T(128)} %stack.23.info, bf16[4,256,1024]{2,1,0:T(8,128)(2,1)} %get-tuple-element.38.qt_ref, f32[4,144,1024]{2,1,0:T(8,128)} %get-tuple-element.39.acc_ref, f32[4,8,1024]{2,1,0:T(8,128)} %get-tuple-element.40.m_ref, bf16[2048,128]{1,0:T(8,128)(2,1)} %copy-done.10, ...), custom_call_target="tpu_custom_call" | custom-call | flops 7516192768 | bytes 4194304 | tf_op jit(solution)/shard_map/attend/pallas_call | solution.py:217
  123.6 1.1 collective-permute-start.20
  124.7 0.7 copy-done.6
  125.4 5.6 %project.6 = (bf16[64,3072]{1,0:T(8,128)(2,1)}, bf16[64,3072]{1,0:T(8,128)(2,1)}, bf16[64,3072]{1,0:T(8,128)(2,1)}, bf16[64,3072]{1,0:T(8,128)(2,1)}) custom-call(s32[5]{0:T(128)} %stack.23.info, bf16[256,512]{1,0:T(8,128)(2,1)} %attend.10.a, bf16[256,512]{1,0:T(8,128)(2,1)} %copy-done.6, bf16[512,6144]{1,0:T(8,128)(2,1)} %wa.7, ...), custom_call_target="tpu_custom_call" | custom-call | flops 1610612736 | bytes 9437184 | tf_op jit(solution)/shard_map/project/pallas_call | solution.py:257
  131.4 1.2 collective-permute-start.22
  132.6 1.4 collective-permute-done.13
  134.0 1.2 collective-permute-start.23
  135.8 1.4 collective-permute-start.18
  137.2 5.5 %project.7 = (bf16[128,3072]{1,0:T(8,128)(2,1)}, bf16[128,3072]{1,0:T(8,128)(2,1)}) custom-call(s32[5]{0:T(128)} %stack.23.info, bf16[256,512]{1,0:T(8,128)(2,1)} %attend.11.a, bf16[256,512]{1,0:T(8,128)(2,1)} %copy-done.5, bf16[512,6144]{1,0:T(8,128)(2,1)} %wa.7, bf16[512,6144]{1,0:T(8,128)(2,1)} %collective-permute-done.9.wb), custom_call_target="tpu_custom_call" | custom-call | flops 1610612736 | bytes 9437184 | tf_op jit(solution)/shard_map/project/pallas_call | solution.py:257
  142.8 8.8 %collective-permute-done.21 = bf16[64,3072]{1,0:T(8,128)(2,1)S(1)} collective-permute-done((bf16[64,3072]{1,0:T(8,128)(2,1)}, bf16[64,3072]{1,0:T(8,128)(2,1)S(1)}, u32[]{:S(2)}, u32[]{:S(2)}) %collective-permute-start.21) | collective-permute-done | bytes 393248 | tf_op jit(solution)/shard_map/ppermute | solution.py:302
  152.2 0.8 collective-permute-start.24
  153.0 0.7 collective-permute-start.25
  153.7 6.3 %collective-permute-done.17 = bf16[32,3072]{1,0:T(8,128)(2,1)S(1)} collective-permute-done((bf16[32,3072]{1,0:T(8,128)(2,1)S(1)}, bf16[32,3072]{1,0:T(8,128)(2,1)S(1)}, u32[]{:S(2)}, u32[]{:S(2)}) %collective-permute-start.17) | collective-permute-done | bytes 196640 | tf_op jit(solution)/shard_map/ppermute | solution.py:302
  160.6 13.1 %collective-permute-done.25 = bf16[128,3072]{1,0:T(8,128)(2,1)S(1)} collective-permute-done((bf16[128,3072]{1,0:T(8,128)(2,1)S(1)}, bf16[128,3072]{1,0:T(8,128)(2,1)S(1)}, u32[]{:S(2)}, u32[]{:S(2)}) %collective-permute-start.25) | collective-permute-done | bytes 786464 | tf_op jit(solution)/shard_map/ppermute | solution.py:302
  173.9 1.9 collective-permute-start.26
  175.8 4.2 %collective-permute-start.27 = (bf16[32,3072]{1,0:T(8,128)(2,1)S(1)}, bf16[32,3072]{1,0:T(8,128)(2,1)S(1)}, u32[]{:S(2)}, u32[]{:S(2)}) collective-permute-start(bf16[32,3072]{1,0:T(8,128)(2,1)S(1)} %get-tuple-element.78), channel_id=1, source_target_pairs={{0,8},{1,9},{2,10},{3,11},{4,12},{5,13},{6,14},{7,15},{8,0},{9,1},... | collective-permute-start | bytes 589832 | tf_op jit(solution)/shard_map/ppermute | solution.py:302
  180.0 2.6 %collective-permute-done.26 = bf16[32,3072]{1,0:T(8,128)(2,1)S(1)} collective-permute-done((bf16[32,3072]{1,0:T(8,128)(2,1)S(1)}, bf16[32,3072]{1,0:T(8,128)(2,1)S(1)}, u32[]{:S(2)}, u32[]{:S(2)}) %collective-permute-start.26) | collective-permute-done | bytes 196640 | tf_op jit(solution)/shard_map/ppermute | solution.py:302
  182.6 5.1 %collective-permute-done.27 = bf16[32,3072]{1,0:T(8,128)(2,1)S(1)} collective-permute-done((bf16[32,3072]{1,0:T(8,128)(2,1)S(1)}, bf16[32,3072]{1,0:T(8,128)(2,1)S(1)}, u32[]{:S(2)}, u32[]{:S(2)}) %collective-permute-start.27) | collective-permute-done | bytes 196640 | tf_op jit(solution)/shard_map/ppermute | solution.py:302
  187.9 2.5 %collective-permute-start.29 = (bf16[64,3072]{1,0:T(8,128)(2,1)S(1)}, bf16[64,3072]{1,0:T(8,128)(2,1)S(1)}, u32[]{:S(2)}, u32[]{:S(2)}) collective-permute-start(bf16[64,3072]{1,0:T(8,128)(2,1)S(1)} %pad_maximum_fusion.2), channel_id=1, source_target_pairs={{0,1},{1,0},{2,3},{3,2},{4,5},{5,4},{6,7},{7,6},{8,9},{9,8},{10,11... | collective-permute-start | bytes 1179656 | tf_op jit(solution)/shard_map/ppermute | solution.py:302
  190.3 1.3 collective-permute-done.29
  191.8 0.9 pad_maximum_fusion
  (80 shorter events, 5.1 us)
Async XLA Ops:
  3.2 10.8 %copy-start.2 = (bf16[2048,128]{1,0:T(8,128)(2,1)S(1)}, bf16[2048,128]{1,0:T(8,128)(2,1)}, u32[]{:S(2)}) copy-start(bf16[2048,128]{1,0:T(8,128)(2,1)} %prep.1.kv_ref) | copy-start | bytes 1572868
  13.4 68.6 %collective-permute-start.9 = (bf16[512,6144]{1,0:T(8,128)(2,1)}, bf16[512,6144]{1,0:T(8,128)(2,1)}, u32[]{:S(2)}, u32[]{:S(2)}) collective-permute-start(bf16[512,6144]{1,0:T(8,128)(2,1)} %wa.7), channel_id=1, source_target_pairs={{0,1},{1,0},{2,3},{3,2},{4,5},{5,4},{6,7},{7,6},{8,9},{9,8},{10,11... | collective-permute-start | bytes 18874376 | tf_op jit(solution)/shard_map/ppermute | solution.py:302
  14.0 15.4 %collective-permute-start = (bf16[2048,128]{1,0:T(8,128)(2,1)S(1)}, bf16[2048,128]{1,0:T(8,128)(2,1)S(1)}, u32[]{:S(2)}, u32[]{:S(2)}) collective-permute-start(bf16[2048,128]{1,0:T(8,128)(2,1)S(1)} %copy-done.2), channel_id=1, source_target_pairs={{0,16},{1,33},{2,18},{3,35},{4,20},{5,37},{6,22},{7,39},{8,24},{9,... | collective-permute-start | bytes 1572872 | tf_op jit(solution)/shard_map/ppermute | solution.py:313
  15.3 16.9 %collective-permute-start.1 = (bf16[2048,128]{1,0:T(8,128)(2,1)S(1)}, bf16[2048,128]{1,0:T(8,128)(2,1)S(1)}, u32[]{:S(2)}, u32[]{:S(2)}) collective-permute-start(bf16[2048,128]{1,0:T(8,128)(2,1)S(1)} %copy-done.2), channel_id=1, source_target_pairs={{0,48},{1,65},{2,50},{3,67},{4,52},{5,69},{6,54},{7,71},{8,56},{9,... | collective-permute-start | bytes 1572872 | tf_op jit(solution)/shard_map/ppermute | solution.py:313
  29.4 5.1 %copy-start.10 = (bf16[2048,128]{1,0:T(8,128)(2,1)}, bf16[2048,128]{1,0:T(8,128)(2,1)S(1)}, u32[]{:S(2)}) copy-start(bf16[2048,128]{1,0:T(8,128)(2,1)S(1)} %collective-permute-done.refs_0_) | copy-start | bytes 1572868
  29.4 4.9 %collective-permute-start.2 = (bf16[2048,128]{1,0:T(8,128)(2,1)S(1)}, bf16[2048,128]{1,0:T(8,128)(2,1)S(1)}, u32[]{:S(2)}, u32[]{:S(2)}) collective-permute-start(bf16[2048,128]{1,0:T(8,128)(2,1)S(1)} %collective-permute-done.refs_0_), channel_id=1, source_target_pairs={{0,1},{1,0},{2,3},{3,2},{4,5},{5,4},{6,7},{7,6},{8,9},{9,8},{10,11... | collective-permute-start | bytes 1572872 | tf_op jit(solution)/shard_map/ppermute | solution.py:302
  32.2 2.3 %copy-start.11 = (bf16[2048,128]{1,0:T(8,128)(2,1)}, bf16[2048,128]{1,0:T(8,128)(2,1)S(1)}, u32[]{:S(2)}) copy-start(bf16[2048,128]{1,0:T(8,128)(2,1)S(1)} %collective-permute-done.1.refs_1_) | copy-start | bytes 1572868
  32.2 2.3 %collective-permute-start.3 = (bf16[2048,128]{1,0:T(8,128)(2,1)S(1)}, bf16[2048,128]{1,0:T(8,128)(2,1)S(1)}, u32[]{:S(2)}, u32[]{:S(2)}) collective-permute-start(bf16[2048,128]{1,0:T(8,128)(2,1)S(1)} %collective-permute-done.1.refs_1_), channel_id=1, source_target_pairs={{0,1},{1,0},{2,3},{3,2},{4,5},{5,4},{6,7},{7,6},{8,9},{9,8},{10,11... | collective-permute-start | bytes 1572872 | tf_op jit(solution)/shard_map/ppermute | solution.py:302
  32.3 20.7 %collective-permute-start.4 = (bf16[2048,128]{1,0:T(8,128)(2,1)S(1)}, bf16[2048,128]{1,0:T(8,128)(2,1)S(1)}, u32[]{:S(2)}, u32[]{:S(2)}) collective-permute-start(bf16[2048,128]{1,0:T(8,128)(2,1)S(1)} %copy-done.2), channel_id=1, source_target_pairs={{0,80},{1,97},{2,82},{3,99},{4,84},{5,101},{6,86},{7,103},{8,88},{... | collective-permute-start | bytes 1572872 | tf_op jit(solution)/shard_map/ppermute | solution.py:313
  33.6 19.4 %collective-permute-start.5 = (bf16[2048,128]{1,0:T(8,128)(2,1)S(1)}, bf16[2048,128]{1,0:T(8,128)(2,1)S(1)}, u32[]{:S(2)}, u32[]{:S(2)}) collective-permute-start(bf16[2048,128]{1,0:T(8,128)(2,1)S(1)} %copy-done.2), channel_id=1, source_target_pairs={{0,112},{2,114},{4,116},{6,118},{8,120},{10,122},{12,124},{14,126}} | collective-permute-start | bytes 1572872 | tf_op jit(solution)/shard_map/ppermute | solution.py:313
  34.3 0.8 copy-start.12
  34.5 0.8 copy-start.13
  53.0 13.2 %copy-start.14 = (bf16[2048,128]{1,0:T(8,128)(2,1)}, bf16[2048,128]{1,0:T(8,128)(2,1)S(1)}, u32[]{:S(2)}) copy-start(bf16[2048,128]{1,0:T(8,128)(2,1)S(1)} %collective-permute-done.4.refs_0_.refs_2_) | copy-start | bytes 1572868
  53.0 13.2 %collective-permute-start.6 = (bf16[2048,128]{1,0:T(8,128)(2,1)S(1)}, bf16[2048,128]{1,0:T(8,128)(2,1)S(1)}, u32[]{:S(2)}, u32[]{:S(2)}) collective-permute-start(bf16[2048,128]{1,0:T(8,128)(2,1)S(1)} %collective-permute-done.4.refs_0_.refs_2_), channel_id=1, source_target_pairs={{0,1},{1,0},{2,3},{3,2},{4,5},{5,4},{6,7},{7,6},{8,9},{9,8},{10,11... | collective-permute-start | bytes 1572872 | tf_op jit(solution)/shard_map/ppermute | solution.py:302
  53.1 13.2 %copy-start.15 = (bf16[2048,128]{1,0:T(8,128)(2,1)}, bf16[2048,128]{1,0:T(8,128)(2,1)S(1)}, u32[]{:S(2)}) copy-start(bf16[2048,128]{1,0:T(8,128)(2,1)S(1)} %collective-permute-done.5.refs_1_.refs_3_) | copy-start | bytes 1572868
  53.1 13.2 %collective-permute-start.7 = (bf16[2048,128]{1,0:T(8,128)(2,1)S(1)}, bf16[2048,128]{1,0:T(8,128)(2,1)S(1)}, u32[]{:S(2)}, u32[]{:S(2)}) collective-permute-start(bf16[2048,128]{1,0:T(8,128)(2,1)S(1)} %collective-permute-done.5.refs_1_.refs_3_), channel_id=1, source_target_pairs={{0,1},{1,0},{2,3},{3,2},{4,5},{5,4},{6,7},{7,6},{8,9},{9,8},{10,11... | collective-permute-start | bytes 1572872 | tf_op jit(solution)/shard_map/ppermute | solution.py:302
  66.3 0.8 copy-start.16
  67.1 0.8 copy-start.17
  74.2 7.7 %collective-permute-start.8 = (bf16[256,512]{1,0:T(8,128)(2,1)}, bf16[256,512]{1,0:T(8,128)(2,1)S(1)}, u32[]{:S(2)}, u32[]{:S(2)}) collective-permute-start(bf16[256,512]{1,0:T(8,128)(2,1)} %attend.8.a), channel_id=1, source_target_pairs={{0,1},{1,0},{2,3},{3,2},{4,5},{5,4},{6,7},{7,6},{8,9},{9,8},{10,11... | collective-permute-start | bytes 786440 | tf_op jit(solution)/shard_map/ppermute | solution.py:302
  81.8 22.8 %collective-permute-start.14 = (bf16[256,512]{1,0:T(8,128)(2,1)}, bf16[256,512]{1,0:T(8,128)(2,1)S(1)}, u32[]{:S(2)}, u32[]{:S(2)}) collective-permute-start(bf16[256,512]{1,0:T(8,128)(2,1)} %attend.9.a), channel_id=1, source_target_pairs={{0,1},{1,0},{2,3},{3,2},{4,5},{5,4},{6,7},{7,6},{8,9},{9,8},{10,11... | collective-permute-start | bytes 786440 | tf_op jit(solution)/shard_map/ppermute | solution.py:302
  81.9 0.7 copy-start.8
  88.2 23.9 %collective-permute-start.10 = (bf16[64,3072]{1,0:T(8,128)(2,1)}, bf16[64,3072]{1,0:T(8,128)(2,1)S(1)}, u32[]{:S(2)}, u32[]{:S(2)}) collective-permute-start(bf16[64,3072]{1,0:T(8,128)(2,1)} %get-tuple-element.53), channel_id=1, source_target_pairs={{0,4},{1,5},{2,6},{3,7},{4,8},{5,9},{6,10},{7,11},{8,12},{9,13},{1... | collective-permute-start | bytes 1179656 | tf_op jit(solution)/shard_map/ppermute | solution.py:302
  88.8 23.3 %collective-permute-start.11 = (bf16[64,3072]{1,0:T(8,128)(2,1)}, bf16[64,3072]{1,0:T(8,128)(2,1)S(1)}, u32[]{:S(2)}, u32[]{:S(2)}) collective-permute-start(bf16[64,3072]{1,0:T(8,128)(2,1)} %get-tuple-element.54), channel_id=1, source_target_pairs={{0,8},{1,9},{2,10},{3,11},{4,12},{5,13},{6,14},{7,15},{8,0},{9,1},... | collective-permute-start | bytes 1179656 | tf_op jit(solution)/shard_map/ppermute | solution.py:302
  91.5 20.7 %collective-permute-start.12 = (bf16[64,3072]{1,0:T(8,128)(2,1)}, bf16[64,3072]{1,0:T(8,128)(2,1)S(1)}, u32[]{:S(2)}, u32[]{:S(2)}) collective-permute-start(bf16[64,3072]{1,0:T(8,128)(2,1)} %get-tuple-element.55), channel_id=1, source_target_pairs={{0,12},{1,13},{2,14},{3,15},{4,0},{5,1},{6,2},{7,3},{8,4},{9,5},{1... | collective-permute-start | bytes 1179656 | tf_op jit(solution)/shard_map/ppermute | solution.py:302
  104.5 7.6 %copy-start.4 = (bf16[64,3072]{1,0:T(8,128)(2,1)S(1)}, bf16[64,3072]{1,0:T(8,128)(2,1)}, u32[]{:S(2)}) copy-start(bf16[64,3072]{1,0:T(8,128)(2,1)} %get-tuple-element.52) | copy-start | bytes 1179652
  104.6 20.2 %collective-permute-start.15 = (bf16[256,512]{1,0:T(8,128)(2,1)}, bf16[256,512]{1,0:T(8,128)(2,1)S(1)}, u32[]{:S(2)}, u32[]{:S(2)}) collective-permute-start(bf16[256,512]{1,0:T(8,128)(2,1)} %attend.10.a), channel_id=1, source_target_pairs={{0,1},{1,0},{2,3},{3,2},{4,5},{5,4},{6,7},{7,6},{8,9},{9,8},{10,11... | collective-permute-start | bytes 786440 | tf_op jit(solution)/shard_map/ppermute | solution.py:302
  104.7 0.7 copy-start.7
  110.9 24.3 %collective-permute-start.16 = (bf16[128,3072]{1,0:T(8,128)(2,1)}, bf16[128,3072]{1,0:T(8,128)(2,1)S(1)}, u32[]{:S(2)}, u32[]{:S(2)}) collective-permute-start(bf16[128,3072]{1,0:T(8,128)(2,1)} %get-tuple-element.63), channel_id=1, source_target_pairs={{0,2},{1,3},{2,0},{3,1},{4,6},{5,7},{6,4},{7,5},{8,10},{9,11},{10,... | collective-permute-start | bytes 2359304 | tf_op jit(solution)/shard_map/ppermute | solution.py:302
  112.4 21.6 %collective-permute-start.13 = (bf16[32,3072]{1,0:T(8,128)(2,1)S(1)}, bf16[32,3072]{1,0:T(8,128)(2,1)S(1)}, u32[]{:S(2)}, u32[]{:S(2)}) collective-permute-start(bf16[32,3072]{1,0:T(8,128)(2,1)S(1)} %slice.97), channel_id=1, source_target_pairs={{0,2},{1,3},{2,0},{3,1},{4,6},{5,7},{6,4},{7,5},{8,10},{9,11},{10,... | collective-permute-start | bytes 589832 | tf_op jit(solution)/shard_map/ppermute | solution.py:302
  123.6 11.7 %copy-start = (bf16[128,3072]{1,0:T(8,128)(2,1)S(1)}, bf16[128,3072]{1,0:T(8,128)(2,1)}, u32[]{:S(2)}) copy-start(bf16[128,3072]{1,0:T(8,128)(2,1)} %get-tuple-element.62) | copy-start | bytes 2359300
  123.6 12.3 %collective-permute-start.20 = (bf16[256,512]{1,0:T(8,128)(2,1)}, bf16[256,512]{1,0:T(8,128)(2,1)S(1)}, u32[]{:S(2)}, u32[]{:S(2)}) collective-permute-start(bf16[256,512]{1,0:T(8,128)(2,1)} %attend.11.a), channel_id=1, source_target_pairs={{0,1},{1,0},{2,3},{3,2},{4,5},{5,4},{6,7},{7,6},{8,9},{9,8},{10,11... | collective-permute-start | bytes 786440 | tf_op jit(solution)/shard_map/ppermute | solution.py:302
  124.7 0.7 copy-start.6
  131.0 20.6 %collective-permute-start.21 = (bf16[64,3072]{1,0:T(8,128)(2,1)}, bf16[64,3072]{1,0:T(8,128)(2,1)S(1)}, u32[]{:S(2)}, u32[]{:S(2)}) collective-permute-start(bf16[64,3072]{1,0:T(8,128)(2,1)} %get-tuple-element.67), channel_id=1, source_target_pairs={{0,4},{1,5},{2,6},{3,7},{4,8},{5,9},{6,10},{7,11},{8,12},{9,13},{1... | collective-permute-start | bytes 1179656 | tf_op jit(solution)/shard_map/ppermute | solution.py:302
  131.4 20.2 %collective-permute-start.22 = (bf16[64,3072]{1,0:T(8,128)(2,1)}, bf16[64,3072]{1,0:T(8,128)(2,1)S(1)}, u32[]{:S(2)}, u32[]{:S(2)}) collective-permute-start(bf16[64,3072]{1,0:T(8,128)(2,1)} %get-tuple-element.68), channel_id=1, source_target_pairs={{0,8},{1,9},{2,10},{3,11},{4,12},{5,13},{6,14},{7,15},{8,0},{9,1},... | collective-permute-start | bytes 1179656 | tf_op jit(solution)/shard_map/ppermute | solution.py:302
  134.0 18.0 %collective-permute-start.23 = (bf16[64,3072]{1,0:T(8,128)(2,1)}, bf16[64,3072]{1,0:T(8,128)(2,1)S(1)}, u32[]{:S(2)}, u32[]{:S(2)}) collective-permute-start(bf16[64,3072]{1,0:T(8,128)(2,1)} %get-tuple-element.69), channel_id=1, source_target_pairs={{0,12},{1,13},{2,14},{3,15},{4,0},{5,1},{6,2},{7,3},{8,4},{9,5},{1... | collective-permute-start | bytes 1179656 | tf_op jit(solution)/shard_map/ppermute | solution.py:302
  135.5 24.6 %collective-permute-start.17 = (bf16[32,3072]{1,0:T(8,128)(2,1)S(1)}, bf16[32,3072]{1,0:T(8,128)(2,1)S(1)}, u32[]{:S(2)}, u32[]{:S(2)}) collective-permute-start(bf16[32,3072]{1,0:T(8,128)(2,1)S(1)} %get-tuple-element.73), channel_id=1, source_target_pairs={{0,4},{1,5},{2,6},{3,7},{4,8},{5,9},{6,10},{7,11},{8,12},{9,13},{1... | collective-permute-start | bytes 589832 | tf_op jit(solution)/shard_map/ppermute | solution.py:302
  135.8 1.4 copy-start.5
  135.8 16.1 %copy-start.3 = (bf16[64,3072]{1,0:T(8,128)(2,1)S(1)}, bf16[64,3072]{1,0:T(8,128)(2,1)}, u32[]{:S(2)}) copy-start(bf16[64,3072]{1,0:T(8,128)(2,1)} %get-tuple-element.66) | copy-start | bytes 1179652
  135.8 24.2 %collective-permute-start.18 = (bf16[32,3072]{1,0:T(8,128)(2,1)S(1)}, bf16[32,3072]{1,0:T(8,128)(2,1)S(1)}, u32[]{:S(2)}, u32[]{:S(2)}) collective-permute-start(bf16[32,3072]{1,0:T(8,128)(2,1)S(1)} %get-tuple-element.75), channel_id=1, source_target_pairs={{0,8},{1,9},{2,10},{3,11},{4,12},{5,13},{6,14},{7,15},{8,0},{9,1},... | collective-permute-start | bytes 589832 | tf_op jit(solution)/shard_map/ppermute | solution.py:302
  142.8 10.2 %copy-start.9 = (bf16[128,3072]{1,0:T(8,128)(2,1)S(1)}, bf16[128,3072]{1,0:T(8,128)(2,1)}, u32[]{:S(2)}) copy-start(bf16[128,3072]{1,0:T(8,128)(2,1)} %get-tuple-element.70) | copy-start | bytes 2359300
  151.6 8.8 %collective-permute-start.19 = (bf16[32,3072]{1,0:T(8,128)(2,1)S(1)}, bf16[32,3072]{1,0:T(8,128)(2,1)S(1)}, u32[]{:S(2)}, u32[]{:S(2)}) collective-permute-start(bf16[32,3072]{1,0:T(8,128)(2,1)S(1)} %get-tuple-element.74), channel_id=1, source_target_pairs={{0,12},{1,13},{2,14},{3,15},{4,0},{5,1},{6,2},{7,3},{8,4},{9,5},{1... | collective-permute-start | bytes 589832 | tf_op jit(solution)/shard_map/ppermute | solution.py:302
  152.1 21.5 %copy-start.1 = (bf16[128,3072]{1,0:T(8,128)(2,1)S(1)}, bf16[128,3072]{1,0:T(8,128)(2,1)}, u32[]{:S(2)}) copy-start(bf16[128,3072]{1,0:T(8,128)(2,1)} %get-tuple-element.65) | copy-start | bytes 2359300
  152.2 8.4 %collective-permute-start.24 = (bf16[32,3072]{1,0:T(8,128)(2,1)S(1)}, bf16[32,3072]{1,0:T(8,128)(2,1)S(1)}, u32[]{:S(2)}, u32[]{:S(2)}) collective-permute-start(bf16[32,3072]{1,0:T(8,128)(2,1)S(1)} %slice.107), channel_id=1, source_target_pairs={{0,2},{1,3},{2,0},{3,1},{4,6},{5,7},{6,4},{7,5},{8,10},{9,11},{10,... | collective-permute-start | bytes 589832 | tf_op jit(solution)/shard_map/ppermute | solution.py:302
  153.0 20.7 %collective-permute-start.25 = (bf16[128,3072]{1,0:T(8,128)(2,1)S(1)}, bf16[128,3072]{1,0:T(8,128)(2,1)S(1)}, u32[]{:S(2)}, u32[]{:S(2)}) collective-permute-start(bf16[128,3072]{1,0:T(8,128)(2,1)S(1)} %copy-done.9), channel_id=1, source_target_pairs={{0,2},{1,3},{2,0},{3,1},{4,6},{5,7},{6,4},{7,5},{8,10},{9,11},{10,... | collective-permute-start | bytes 2359304 | tf_op jit(solution)/shard_map/ppermute | solution.py:302
  173.9 8.7 %collective-permute-start.26 = (bf16[32,3072]{1,0:T(8,128)(2,1)S(1)}, bf16[32,3072]{1,0:T(8,128)(2,1)S(1)}, u32[]{:S(2)}, u32[]{:S(2)}) collective-permute-start(bf16[32,3072]{1,0:T(8,128)(2,1)S(1)} %get-tuple-element.76), channel_id=1, source_target_pairs={{0,4},{1,5},{2,6},{3,7},{4,8},{5,9},{6,10},{7,11},{8,12},{9,13},{1... | collective-permute-start | bytes 589832 | tf_op jit(solution)/shard_map/ppermute | solution.py:302
  175.8 11.9 %collective-permute-start.27 = (bf16[32,3072]{1,0:T(8,128)(2,1)S(1)}, bf16[32,3072]{1,0:T(8,128)(2,1)S(1)}, u32[]{:S(2)}, u32[]{:S(2)}) collective-permute-start(bf16[32,3072]{1,0:T(8,128)(2,1)S(1)} %get-tuple-element.78), channel_id=1, source_target_pairs={{0,8},{1,9},{2,10},{3,11},{4,12},{5,13},{6,14},{7,15},{8,0},{9,1},... | collective-permute-start | bytes 589832 | tf_op jit(solution)/shard_map/ppermute | solution.py:302
  180.0 7.7 %collective-permute-start.28 = (bf16[32,3072]{1,0:T(8,128)(2,1)S(1)}, bf16[32,3072]{1,0:T(8,128)(2,1)S(1)}, u32[]{:S(2)}, u32[]{:S(2)}) collective-permute-start(bf16[32,3072]{1,0:T(8,128)(2,1)S(1)} %get-tuple-element.77), channel_id=1, source_target_pairs={{0,12},{1,13},{2,14},{3,15},{4,0},{5,1},{6,2},{7,3},{8,4},{9,5},{1... | collective-permute-start | bytes 589832 | tf_op jit(solution)/shard_map/ppermute | solution.py:302
  187.9 3.8 %collective-permute-start.29 = (bf16[64,3072]{1,0:T(8,128)(2,1)S(1)}, bf16[64,3072]{1,0:T(8,128)(2,1)S(1)}, u32[]{:S(2)}, u32[]{:S(2)}) collective-permute-start(bf16[64,3072]{1,0:T(8,128)(2,1)S(1)} %pad_maximum_fusion.2), channel_id=1, source_target_pairs={{0,1},{1,0},{2,3},{3,2},{4,5},{5,4},{6,7},{7,6},{8,9},{9,8},{10,11... | collective-permute-start | bytes 1179656 | tf_op jit(solution)/shard_map/ppermute | solution.py:302
